TPU v7x, 512 devices: a whole 4x8x8 slice. The times are simulated.
512 devices in a mesh: dp: 8 (over x, core), row: 4 (over z_hi), col: 16 (over z_lo, y).
Axes of the slice: x: 4, y: 8, z: 8 (z_hi: 4, z_lo: 2; z = z_hi * 2 + z_lo), core: 2. Of those that a mesh axis runs over, the one named last changes fastest.
Arguments:
- activations: bfloat16 [2560, 12288], P(('dp', 'col'), 'row'), may hold values from -24 to 24
- out_grad: bfloat16 [2560, 6144], P(('dp', 'row'), 'col'), may hold values from -2 to 2
- qkv_weight: bfloat16 [12288, 6144], P('row', 'col'), may hold values from -0.0546875 to 0.0546875
Outputs:
- input_grad: bfloat16 [2560, 12288], P(('dp', 'col'), 'row')
- weight_grad: bfloat16 [12288, 6144], P('row', 'col')
All inputs are finite; a program needn't handle non-finite values.
Results may differ from a plain program's by a relative error of at most 0.02.
Values may be sent and summed in bfloat16 or wider, within the bound.
No kernel may reach another device: no remote copies, remote signals or barrier semaphores. Data moves between devices by JAX's collectives and lax.ppermute only.
A program may use at most 64 MiB of HBM per device.

v0:
```python
import jax
import jax.numpy as jnp
from jax import lax
from jax.sharding import PartitionSpec as P


def transposed_product(left, right):
    return lax.dot_general(
        left, right, (((0,), (0,)), ((), ())), preferred_element_type=jnp.float32
    )


def body(activations, out_grad, qkv_weight):
    groups = lax.axis_size("dp")
    grads_all = lax.all_gather(out_grad, "row", axis=0, tiled=True)
    input_grad = lax.psum_scatter(
        lax.dot_general(
            grads_all, qkv_weight, (((1,), (1,)), ((), ())), preferred_element_type=jnp.float32
        ).astype(jnp.bfloat16),
        "col",
        scatter_dimension=0,
        tiled=True,
    )
    group_grad = transposed_product(
        lax.all_gather(activations, "col", axis=0, tiled=True), grads_all
    )
    weight_grad = (
        lax.psum(group_grad.astype(jnp.bfloat16), "dp").astype(jnp.float32) / groups
    ).astype(jnp.bfloat16)
    return (input_grad, weight_grad)


def solution(mesh):
    placed = (P(("dp", "col"), "row"), P(("dp", "row"), "col"), P("row", "col"))
    return jax.shard_map(
        body,
        mesh=mesh,
        in_specs=placed,
        out_specs=(P(("dp", "col"), "row"), P("row", "col")),
        check_vma=False,
    )
```

profile of v0, /device:TPU:1, one launch (start us, length us, event | category | flops | bytes accessed | tf_op | source)
XLA Modules:
  0.0 183.1 jit_solution(1979494650677045315)
XLA Ops:
  7.2 0.0 copy-start
  7.2 0.0 all-gather.3.cloned.1.call-start
  7.2 0.7 all-gather.3.cloned.1.call-update
  7.9 0.0 all-reduce.4.cloned.1.call-start
  8.0 18.6 %all_gather.6 = bf16[320,384]{1,0:T(8,128)(2,1)S(1)} all-gather(bf16[80,384]{1,0:T(8,128)(2,1)} %param.4), channel_id=1, replica_groups=mesh['dp'=8,'row'=4,'col'=16] {'row'}, dimensions={0}, use_global_device_ids=true | all-gather | bytes 307200 | tf_op jit(solution)/shard_map/all_gather | solution.py:15
  26.5 0.0 copy-done
  26.5 2.5 %convolution_convert_fusion.1 = bf16[320,3072]{1,0:T(8,128)(2,1)} fusion(bf16[320,384]{1,0:T(8,128)(2,1)S(1)} %all_gather.6, bf16[3072,384]{1,0:T(8,128)(2,1)S(1)} %copy-done), kind=kOutput, calls=%fused_computation.2 | convolution fusion | flops 755957760 | bytes 4571136 | tf_op jit(solution)/shard_map/dot_general | solution.py:17
  29.0 52.8 %all-gather.3.cloned.1.call-done = bf16[16,20,3072]{2,1,0:T(8,128)(2,1)} async-done(((bf16[1,20,3072]{2,1,0:T(8,128)(2,1)}), bf16[16,20,3072]{2,1,0:T(8,128)(2,1)}) %all-gather.3.cloned.1.call-update) | async-done | bytes 1966096 | tf_op jit(solution)/shard_map/all_gather | solution.py:25
  81.9 4.0 %reshape.5 = bf16[320,3072]{1,0:T(8,128)(2,1)} reshape(bf16[16,20,3072]{2,1,0:T(8,128)(2,1)} %all-gather.3.cloned.1.call-done) | data formatting | bytes 3932160
  85.8 4.6 %convolution_convert_fusion = bf16[3072,384]{1,0:T(8,128)(2,1)} fusion(bf16[320,3072]{1,0:T(8,128)(2,1)} %reshape.5, bf16[320,384]{1,0:T(8,128)(2,1)S(1)} %all_gather.6), kind=kOutput, calls=%fused_computation.1 | convolution fusion | flops 756154368 | bytes 4571136 | tf_op jit(solution)/shard_map/dot_general | solution.py:8
  90.4 0.0 all-reduce.4.cloned.1.call-update
  90.4 38.3 %fusion = bf16[24,3072]{1,0:T(8,128)(2,1)S(1)} fusion(bf16[320,3072]{1,0:T(8,128)(2,1)} %convolution_convert_fusion.1), kind=kCustom, calls=%all-reduce-scatter | all-reduce-scatter fusion | flops 1179649 | bytes 2115584
  128.7 1.3 collective-permute-start
  130.0 2.3 %collective-permute-start.1 = (bf16[24,3072]{1,0:T(8,128)(2,1)S(1)}, bf16[24,3072]{1,0:T(8,128)(2,1)S(1)}, u32[]{:S(2)}, u32[]{:S(2)}) collective-permute-start(bf16[24,3072]{1,0:T(8,128)(2,1)S(1)} %fusion), channel_id=1, source_target_pairs={{0,2},{1,3},{2,4},{3,5},{4,6},{5,7},{6,8},{7,9},{8,10},{9,11},{10,... | collective-permute-start | bytes 442376
  132.4 2.6 %collective-permute-start.2 = (bf16[12,3072]{1,0:T(8,128)(2,1)S(1)}, bf16[12,3072]{1,0:T(8,128)(2,1)S(1)}, u32[]{:S(2)}, u32[]{:S(2)}) collective-permute-start(bf16[12,3072]{1,0:T(8,128)(2,1)S(1)} %slice), channel_id=1, source_target_pairs={{0,3},{1,4},{2,5},{3,6},{4,7},{5,8},{6,9},{7,10},{8,11},{9,12},{10... | collective-permute-start | bytes 221192
  135.0 1.3 dynamic-slice.4
  136.9 1.2 collective-permute-done.2
  138.1 0.0 collective-permute-done
  138.1 0.0 collective-permute-done.1
  138.1 1.0 concatenate
  139.2 0.7 constant_dynamic-slice_fusion
  139.9 32.9 %all-reduce.4.cloned.1.call-done = bf16[3072,384]{1,0:T(8,128)(2,1)} async-done(((bf16[3072,384]{1,0:T(8,128)(2,1)}), bf16[3072,384]{1,0:T(8,128)(2,1)}) %all-reduce.4.cloned.1.call-update) | async-done | bytes 2359312 | tf_op jit(solution)/shard_map/psum | solution.py:28
  172.8 3.5 %multiply_convert_fusion = bf16[3072,384]{1,0:T(8,128)(2,1)} fusion(bf16[3072,384]{1,0:T(8,128)(2,1)} %all-reduce.4.cloned.1.call-done), kind=kLoop, calls=%fused_computation | loop fusion | flops 3538944 | bytes 4718592 | tf_op jit(solution)/shard_map/convert_element_type | solution.py:29
  (1 shorter events, 0.0 us)
Async XLA Ops:
  7.2 19.4 %copy-start = (bf16[3072,384]{1,0:T(8,128)(2,1)S(1)}, bf16[3072,384]{1,0:T(8,128)(2,1)}, u32[]{:S(2)}) copy-start(bf16[3072,384]{1,0:T(8,128)(2,1)} %param.5) | copy-start | bytes 7077892
  7.2 74.7 %all-gather.3.cloned.1.call-start = ((), (), s32[]{:S(2)}) async-start(), calls=%async_computation.1 | async-start | bytes 2506752 | tf_op jit(solution)/shard_map/all_gather | solution.py:25
  7.9 164.8 %all-reduce.4.cloned.1.call-start = ((), (), s32[]{:S(2)}) async-start(), calls=%async_computation | async-start | bytes 4718592 | tf_op jit(solution)/shard_map/psum | solution.py:28
  128.7 9.4 %collective-permute-start = (bf16[24,3072]{1,0:T(8,128)(2,1)S(1)}, bf16[24,3072]{1,0:T(8,128)(2,1)S(1)}, u32[]{:S(2)}, u32[]{:S(2)}) collective-permute-start(bf16[24,3072]{1,0:T(8,128)(2,1)S(1)} %fusion), channel_id=1, source_target_pairs={{0,1},{1,2},{2,3},{3,4},{4,5},{5,6},{6,7},{7,8},{8,9},{9,10},{10,1... | collective-permute-start | bytes 442376
  130.0 8.1 %collective-permute-start.1 = (bf16[24,3072]{1,0:T(8,128)(2,1)S(1)}, bf16[24,3072]{1,0:T(8,128)(2,1)S(1)}, u32[]{:S(2)}, u32[]{:S(2)}) collective-permute-start(bf16[24,3072]{1,0:T(8,128)(2,1)S(1)} %fusion), channel_id=1, source_target_pairs={{0,2},{1,3},{2,4},{3,5},{4,6},{5,7},{6,8},{7,9},{8,10},{9,11},{10,... | collective-permute-start | bytes 442376
  132.4 5.7 %collective-permute-start.2 = (bf16[12,3072]{1,0:T(8,128)(2,1)S(1)}, bf16[12,3072]{1,0:T(8,128)(2,1)S(1)}, u32[]{:S(2)}, u32[]{:S(2)}) collective-permute-start(bf16[12,3072]{1,0:T(8,128)(2,1)S(1)} %slice), channel_id=1, source_target_pairs={{0,3},{1,4},{2,5},{3,6},{4,7},{5,8},{6,9},{7,10},{8,11},{9,12},{10... | collective-permute-start | bytes 221192
Sparse Core Ops, SparseCore 0:
  10.1 71.7 all-gather.2
  90.6 82.1 all-reduce.3
where the time goes:
time: 184 us; the launch traced here: 183 us
  waiting for transfers between devices  87.6 us (48%)
  blocking collectives  56.9 us (31%)
  between operations  14.7 us (8%)
  matrix products  7.09 us (4%)
  local copies, waits for them, and re-layouts  6.99 us (4%)
  starting transfers between devices  6.27 us (3%)
  other arithmetic  3.52 us (2%)
    all_gather x1, waiting for transfers between devices, body(): lax.all_gather(activations, 'col', axis=0, tiled=True)  52.8 us
    unnamed x1, blocking collectives  38.3 us
    psum x1, waiting for transfers between devices, body(): lax.psum(group_grad.astype(jnp.bfloat16), 'dp').astype(jnp.float32) / groups  32.9 us
    all_gather x1, blocking collectives, body(): grads_all = lax.all_gather(out_grad, 'row', axis=0, tiled=True)  18.6 us
    unnamed x7, local copies, waits for them, and re-layouts  6.99 us
    unnamed x3, starting transfers between devices  6.19 us
    dot_general x1, matrix products, transposed_product(): lax.dot_general(left, right, (((0,), (0,)), ((), ())), preferred_element_...  4.6 us
  transfers between devices with their start and end apart: 5, of which 3 were waited for; matrix products, arithmetic and copies ran while one was open for 24% of the time, Pallas kernels for 0%

commit v1 on v0

v1 whole, which is shorter than its diff:
```python
import jax
import jax.numpy as jnp
from jax import lax
from jax.sharding import Mesh, PartitionSpec as P

F32 = jnp.float32
BF16 = jnp.bfloat16


def swap(value, axis):
    return lax.ppermute(value, axis, [(0, 1), (1, 0)])


def around(value, axis, step):
    size = lax.axis_size(axis)
    return lax.ppermute(value, axis, [(i, (i + step) % size) for i in range(size)])


def block(array, index, size):
    return lax.dynamic_slice_in_dim(array, index * size, size, 0)


def token_order(rows, zh, core):
    shape = (rows, rows)
    want = lax.broadcasted_iota(jnp.int32, shape, 0)
    have = lax.broadcasted_iota(jnp.int32, shape, 1)
    unit, inner = want // 20, want % 20
    y, zl, g = unit // 4, (unit // 2) % 2, unit % 2
    part = zl * 2 + y // 4
    source = ((g + core) % 2) * 320 + ((part - zh) % 4) * 80 + (y % 4) * 20 + inner
    return (source == have).astype(BF16)


def body(activations, out_grad, qkv_weight):
    x, core, zh, zl = (lax.axis_index(name) for name in ("x", "core", "zh", "zl"))
    ny = lax.axis_size("y")
    quarters = activations.reshape(20, 4, 768).transpose(1, 0, 2)
    mine = lax.all_to_all(quarters, ("zl", "core"), 0, 0, tiled=True).reshape(80, 768)
    acts = lax.all_to_all(
        jnp.broadcast_to(mine[None], (ny, 80, 768)), "y", 0, 0, tiled=True
    ).reshape(640, 768)
    grads = jnp.concatenate([out_grad, swap(out_grad, "zl")], axis=1)
    grads = jnp.concatenate([grads] + [around(grads, "zh", -k) for k in (1, 2, 3)], axis=0)
    grads = jnp.concatenate([grads, swap(grads, "core")], axis=0)
    grads = lax.dot_general(
        token_order(640, zh, core), grads, (((1,), (0,)), ((), ())), preferred_element_type=F32
    ).astype(BF16)
    weight = jnp.concatenate(
        [
            block(qkv_weight, zl * 2 + core, 768),
            swap(block(qkv_weight, (1 - zl) * 2 + core, 768), "zl"),
        ],
        axis=1,
    )
    parts = lax.dot_general(
        grads, weight, (((1,), (1,)), ((), ())), preferred_element_type=F32
    ).astype(BF16)
    parts = lax.all_to_all(parts.reshape(ny, 80, 768), "y", 0, 0, tiled=True)
    parts = parts.astype(F32).sum(0).astype(BF16)
    input_grad = lax.all_to_all(parts.reshape(4, 20, 768), ("zl", "core"), 0, 0, tiled=True)
    input_grad = input_grad.transpose(1, 0, 2).reshape(20, 3072)
    group = lax.dot_general(
        acts, grads, (((0,), (0,)), ((), ())), preferred_element_type=F32
    ).astype(BF16)
    total = block(group, x, 192).astype(F32)
    for k in (1, 2, 3):
        total += around(block(group, (x + k) % 4, 192), "x", k).astype(F32)
    total = (total / 8).astype(BF16)
    own, other = total[:, :384], total[:, 384:]
    pair = jnp.stack([jnp.where(zl == 0, own, other), jnp.where(zl == 0, other, own)])
    spread = jnp.broadcast_to(pair[None], (4, 2, 192, 384)).reshape(8, 192, 384)
    half = lax.all_to_all(spread, ("x", "zl"), 0, 0, tiled=True)
    half = half.reshape(4, 2, 192, 384).transpose(1, 0, 2, 3).reshape(2, 768, 384)
    other_half = swap(half, "core")
    first = jnp.where(core == 0, half, other_half)
    second = jnp.where(core == 0, other_half, half)
    weight_grad = jnp.stack([first, second], axis=1).reshape(3072, 384)
    return input_grad, weight_grad


def solution(mesh):
    fine = Mesh(mesh.devices.reshape(4, 2, 4, 2, 8), ("x", "core", "zh", "zl", "y"))
    tokens, grads, features = P(("x", "core", "zl", "y"), "zh"), P(("x", "core", "zh"), ("zl", "y")), P("zh", ("zl", "y"))
    return jax.shard_map(
        body,
        mesh=fine,
        in_specs=(tokens, grads, features),
        out_specs=(tokens, features),
        check_vma=False,
    )
```

time: 184 us -> 170 us (0.924)
  starting transfers between devices: 6.27 us -> 70.5 us
  blocking collectives: 56.9 us -> 0 us
  between operations: 14.7 us -> 0.96 us
  waiting for transfers between devices: 87.6 us -> 80.2 us
  other arithmetic: 3.52 us -> 1.04 us
    all_gather x1 -> x0, waiting for transfers between devices: 52.8 us -> none  [body(): lax.all_gather(activations, 'col', axis=0, tiled=True)]
    all_to_all x0 -> x5, waiting for transfers between devices: none -> 47.7 us  [the longest x1 23.6 us: body(): lax.all_to_all(jnp.broadcast_to(mine[None], (ny, 80, 768)), 'y', 0, 0, ti...]
    ppermute x0 -> x10, starting transfers between devices: none -> 43.4 us  [the longest x6 27.3 us: around(): lax.ppermute(value, axis, [(i, (i + step) % size) for i in range(size)])]
    unnamed x1 -> x0, blocking collectives: 38.3 us -> none
    psum x1 -> x0, waiting for transfers between devices: 32.9 us -> none  [body(): lax.psum(group_grad.astype(jnp.bfloat16), 'dp').astype(jnp.float32) / groups]
    ppermute x0 -> x10, waiting for transfers between devices: none -> 32.5 us  [the longest x4 22.9 us: swap(): return lax.ppermute(value, axis, [(0, 1), (1, 0)])]
    all_to_all x0 -> x5, starting transfers between devices: none -> 27.1 us  [the longest x1 6.82 us: body(): lax.all_to_all(jnp.broadcast_to(mine[None], (ny, 80, 768)), 'y', 0, 0, ti...]
    all_gather x1 -> x0, blocking collectives: 18.6 us -> none  [body(): grads_all = lax.all_gather(out_grad, 'row', axis=0, tiled=True)]
  transfers between devices with their start and end apart: 5 -> 15, of which waited for: 3 -> 9; matrix products, arithmetic and copies ran while one was open for 24% -> 7% of each run, Pallas kernels for 0% -> 0%
where the time goes in v1:
time: 170 us; the launch traced here: 169 us
  waiting for transfers between devices  80.2 us (47%)
  starting transfers between devices  70.5 us (41%)
  matrix products  8.33 us (5%)
  local copies, waits for them, and re-layouts  8.19 us (5%)
    ppermute x6, starting transfers between devices, around(): lax.ppermute(value, axis, [(i, (i + step) % size) for i in range(size)])  27.3 us
    all_to_all x1, waiting for transfers between devices, body(): lax.all_to_all(jnp.broadcast_to(mine[None], (ny, 80, 768)), 'y', 0, 0, ti...  23.6 us
    ppermute x4, waiting for transfers between devices, swap(): return lax.ppermute(value, axis, [(0, 1), (1, 0)])  22.9 us
    all_to_all x1, waiting for transfers between devices, body(): parts = lax.all_to_all(parts.reshape(ny, 80, 768), 'y', 0, 0, tiled=True)  20.3 us
    ppermute x4, starting transfers between devices, swap(): return lax.ppermute(value, axis, [(0, 1), (1, 0)])  16.1 us
    ppermute x6, waiting for transfers between devices, around(): lax.ppermute(value, axis, [(i, (i + step) % size) for i in range(size)])  9.63 us
    all_to_all x1, starting transfers between devices, body(): lax.all_to_all(jnp.broadcast_to(mine[None], (ny, 80, 768)), 'y', 0, 0, ti...  6.82 us
    all_to_all x1, starting transfers between devices, body(): lax.all_to_all(parts.reshape(4, 20, 768), ('zl', 'core'), 0, 0, tiled=True)  6.15 us
  transfers between devices with their start and end apart: 15, of which 9 were waited for; matrix products, arithmetic and copies ran while one was open for 7% of the time, Pallas kernels for 0%

profile of v1, /device:TPU:1, one launch (start us, length us, event | category | flops | bytes accessed | tf_op | source)
XLA Modules:
  0.0 169.2 jit_solution(17867485612542107922)
XLA Ops:
  0.6 4.8 %collective-permute-start = (bf16[80,384]{1,0:T(8,128)(2,1)}, bf16[80,384]{1,0:T(8,128)(2,1)S(1)}, u32[]{:S(2)}, u32[]{:S(2)}) collective-permute-start(bf16[80,384]{1,0:T(8,128)(2,1)} %param.4), channel_id=1, source_target_pairs={{0,8},{8,0},{1,9},{9,1},{2,10},{10,2},{3,11},{11,3},{4,12},{12,4},... | collective-permute-start | bytes 184328 | tf_op jit(solution)/shard_map/ppermute | solution.py:11
  5.5 0.9 constant_dynamic-update-slice_fusion.1
  6.3 1.0 collective-permute-done
  7.3 5.8 %collective-permute-start.3 = (bf16[80,768]{1,0:T(8,128)(2,1)S(1)}, bf16[80,768]{1,0:T(8,128)(2,1)S(1)}, u32[]{:S(2)}, u32[]{:S(2)}) collective-permute-start(bf16[80,768]{1,0:T(8,128)(2,1)S(1)} %get-tuple-element.11), channel_id=1, source_target_pairs={{0,16},{16,32},{32,48},{48,0},{1,17},{17,33},{33,49},{49,1},{2,18}... | collective-permute-start | bytes 368648 | tf_op jit(solution)/shard_map/ppermute | solution.py:16
  13.1 8.2 %collective-permute-start.2 = (bf16[80,768]{1,0:T(8,128)(2,1)S(1)}, bf16[80,768]{1,0:T(8,128)(2,1)S(1)}, u32[]{:S(2)}, u32[]{:S(2)}) collective-permute-start(bf16[80,768]{1,0:T(8,128)(2,1)S(1)} %get-tuple-element.11), channel_id=1, source_target_pairs={{0,32},{16,48},{32,0},{48,16},{1,33},{17,49},{33,1},{49,17},{2,34}... | collective-permute-start | bytes 368648 | tf_op jit(solution)/shard_map/ppermute | solution.py:16
  21.3 3.4 %collective-permute-start.1 = (bf16[80,768]{1,0:T(8,128)(2,1)S(1)}, bf16[80,768]{1,0:T(8,128)(2,1)S(1)}, u32[]{:S(2)}, u32[]{:S(2)}) collective-permute-start(bf16[80,768]{1,0:T(8,128)(2,1)S(1)} %get-tuple-element.11), channel_id=1, source_target_pairs={{0,48},{16,0},{32,16},{48,32},{1,49},{17,1},{33,17},{49,33},{2,50}... | collective-permute-start | bytes 368648 | tf_op jit(solution)/shard_map/ppermute | solution.py:16
  24.7 1.0 reshape.36
  26.4 6.0 %all-to-all-start.2 = ((bf16[4,20,768]{2,1,0:T(8,128)(2,1)}), bf16[4,20,768]{2,1,0:T(8,128)(2,1)S(1)}, u32[]{:S(2)}, u32[]{:S(2)}) async-start(bf16[4,20,768]{2,1,0:T(8,128)(2,1)} %bitcast.44), calls=%async_computation.2 | async-start | bytes 294912 | tf_op jit(solution)/shard_map/all_to_all | solution.py:38
  32.4 1.2 collective-permute-done.1
  33.6 2.9 %collective-permute-start.4 = (bf16[320,768]{1,0:T(8,128)(2,1)S(1)}, bf16[320,768]{1,0:T(8,128)(2,1)S(1)}, u32[]{:S(2)}, u32[]{:S(2)}) collective-permute-start(bf16[320,768]{1,0:T(8,128)(2,1)S(1)} %pad_maximum_fusion.1), channel_id=1, source_target_pairs={{0,64},{64,0},{1,65},{65,1},{2,66},{66,2},{3,67},{67,3},{4,68},{68... | collective-permute-start | bytes 1474568 | tf_op jit(solution)/shard_map/ppermute | solution.py:11
  36.6 1.0 broadcast_in_dim.14
  37.6 6.8 %all-to-all-start.3 = ((bf16[8,80,768]{2,1,0:T(8,128)(2,1)}), bf16[8,80,768]{2,1,0:T(8,128)(2,1)S(1)}, u32[]{:S(2)}, u32[]{:S(2)}) async-start(bf16[8,80,768]{2,1,0:T(8,128)(2,1)} %broadcast_in_dim.14), calls=%async_computation.3 | async-start | bytes 1966080 | tf_op jit(solution)/shard_map/all_to_all | solution.py:39
  44.6 4.0 %fusion.24 = bf16[640,768]{1,0:T(8,128)(2,1)} fusion(bf16[640,768]{1,0:T(8,128)(2,1)S(1)} %constant_dynamic-update-slice_fusion.2, s32[640]{0:T(1024)S(1)} %get-tuple-element.16, s32[640]{0:T(1024)S(1)} %get-tuple-element.17, s32[]{:T(128)S(6)} %axis_index.48, s32[]{:T(128)S(6)} %axis_index.45, s32[640]{0:T(1024)S(1)} %get-tuple-element.15, ...), kind=kOutput, calls=%fused_computation.51 | convolution fusion | flops 668139520 | bytes 1977608 | tf_op jit(solution)/shard_map/dot_general | solution.py:45
  48.6 23.6 %all-to-all-done.3 = bf16[8,80,768]{2,1,0:T(8,128)(2,1)S(1)} async-done(((bf16[8,80,768]{2,1,0:T(8,128)(2,1)}), bf16[8,80,768]{2,1,0:T(8,128)(2,1)S(1)}, u32[]{:S(2)}, u32[]{:S(2)}) %all-to-all-start.3) | async-done | bytes 983072 | tf_op jit(solution)/shard_map/all_to_all | solution.py:39
  72.2 2.3 %convolution_convert_fusion = bf16[768,768]{0,1:T(8,128)(2,1)S(1)} fusion(bf16[640,768]{1,0:T(8,128)(2,1)} %fusion.24, bf16[640,768]{1,0:T(8,128)(2,1)S(1)} %bitcast.48), kind=kOutput, calls=%fused_computation.50 | convolution fusion | flops 755564544 | bytes 3145728 | tf_op jit(solution)/shard_map/dot_general | solution.py:62
  74.7 3.1 %collective-permute-start.6 = (bf16[192,768]{1,0:T(8,128)(2,1)S(1)}, bf16[192,768]{1,0:T(8,128)(2,1)S(1)}, u32[]{:S(2)}, u32[]{:S(2)}) collective-permute-start(bf16[192,768]{1,0:T(8,128)(2,1)S(1)} %get-tuple-element.6), channel_id=1, source_target_pairs={{0,128},{128,256},{256,384},{384,0},{1,129},{129,257},{257,385},{3... | collective-permute-start | bytes 884744 | tf_op jit(solution)/shard_map/ppermute | solution.py:16
  77.8 3.4 %collective-permute-start.8 = (bf16[192,768]{1,0:T(8,128)(2,1)S(1)}, bf16[192,768]{1,0:T(8,128)(2,1)S(1)}, u32[]{:S(2)}, u32[]{:S(2)}) collective-permute-start(bf16[192,768]{1,0:T(8,128)(2,1)S(1)} %get-tuple-element.7), channel_id=1, source_target_pairs={{0,384},{128,0},{256,128},{384,256},{1,385},{129,1},{257,129},{385... | collective-permute-start | bytes 884744 | tf_op jit(solution)/shard_map/ppermute | solution.py:16
  81.2 3.4 %collective-permute-start.7 = (bf16[192,768]{1,0:T(8,128)(2,1)S(1)}, bf16[192,768]{1,0:T(8,128)(2,1)S(1)}, u32[]{:S(2)}, u32[]{:S(2)}) collective-permute-start(bf16[192,768]{1,0:T(8,128)(2,1)S(1)} %get-tuple-element.8), channel_id=1, source_target_pairs={{0,256},{128,384},{256,0},{384,128},{1,257},{129,385},{257,1},{385... | collective-permute-start | bytes 884744 | tf_op jit(solution)/shard_map/ppermute | solution.py:16
  84.6 1.2 collective-permute-done.6
  85.8 1.6 collective-permute-done.8
  87.4 5.6 %collective-permute-done.7 = bf16[192,768]{1,0:T(8,128)(2,1)S(1)} collective-permute-done((bf16[192,768]{1,0:T(8,128)(2,1)S(1)}, bf16[192,768]{1,0:T(8,128)(2,1)S(1)}, u32[]{:S(2)}, u32[]{:S(2)}) %collective-permute-start.7) | collective-permute-done | bytes 294944 | tf_op jit(solution)/shard_map/ppermute | solution.py:16
  93.3 1.1 broadcast_in_dim.15
  94.4 4.6 %all-to-all-start.4 = ((bf16[8,192,384]{2,1,0:T(8,128)(2,1)}), bf16[8,192,384]{2,1,0:T(8,128)(2,1)S(1)}, u32[]{:S(2)}, u32[]{:S(2)}) async-start(bf16[8,192,384]{2,1,0:T(8,128)(2,1)} %bitcast.10), calls=%async_computation.4 | async-start | bytes 2359296 | tf_op jit(solution)/shard_map/all_to_all | solution.py:72
  99.1 3.5 %collective-permute-start.5 = (bf16[768,384]{1,0:T(8,128)(2,1)S(1)}, bf16[768,384]{1,0:T(8,128)(2,1)S(1)}, u32[]{:S(2)}, u32[]{:S(2)}) collective-permute-start(bf16[768,384]{1,0:T(8,128)(2,1)S(1)} %get-tuple-element.5), channel_id=1, source_target_pairs={{0,8},{8,0},{1,9},{9,1},{2,10},{10,2},{3,11},{11,3},{4,12},{12,4},... | collective-permute-start | bytes 1769480 | tf_op jit(solution)/shard_map/ppermute | solution.py:11
  102.6 21.9 %collective-permute-done.5 = bf16[768,384]{1,0:T(8,128)(2,1)S(1)} collective-permute-done((bf16[768,384]{1,0:T(8,128)(2,1)S(1)}, bf16[768,384]{1,0:T(8,128)(2,1)S(1)}, u32[]{:S(2)}, u32[]{:S(2)}) %collective-permute-start.5) | collective-permute-done | bytes 589856 | tf_op jit(solution)/shard_map/ppermute | solution.py:11
  124.6 1.9 %convolution_convert_fusion.1 = bf16[640,768]{1,0:T(8,128)(2,1)} fusion(bf16[640,768]{1,0:T(8,128)(2,1)S(1)} %copy-done.1, bf16[768,384]{1,0:T(8,128)(2,1)S(1)} %collective-permute-done.5, bf16[768,384]{1,0:T(8,128)(2,1)S(1)} %get-tuple-element.4), kind=kOutput, calls=%fused_computation.52 | convolution fusion | flops 757825536 | bytes 3145728 | tf_op jit(solution)/shard_map/dot_general | solution.py:55
  126.5 3.6 %all-to-all-start = ((bf16[8,80,768]{2,1,0:T(8,128)(2,1)}), bf16[8,80,768]{2,1,0:T(8,128)(2,1)S(1)}, u32[]{:S(2)}, u32[]{:S(2)}) async-start(bf16[8,80,768]{2,1,0:T(8,128)(2,1)} %bitcast), calls=%async_computation | async-start | bytes 1966080 | tf_op jit(solution)/shard_map/all_to_all | solution.py:58
  130.2 5.0 %collective-permute-start.9 = (bf16[2,768,384]{2,1,0:T(8,128)(2,1)S(1)}, bf16[2,768,384]{2,1,0:T(8,128)(2,1)S(1)}, u32[]{:S(2)}, u32[]{:S(2)}) collective-permute-start(bf16[2,768,384]{2,1,0:T(8,128)(2,1)S(1)} %bitcast.45), channel_id=1, source_target_pairs={{0,64},{64,0},{1,65},{65,1},{2,66},{66,2},{3,67},{67,3},{4,68},{68... | collective-permute-start | bytes 3538952 | tf_op jit(solution)/shard_map/ppermute | solution.py:11
  135.2 20.3 %all-to-all-done = bf16[8,80,768]{2,1,0:T(8,128)(2,1)S(1)} async-done(((bf16[8,80,768]{2,1,0:T(8,128)(2,1)}), bf16[8,80,768]{2,1,0:T(8,128)(2,1)S(1)}, u32[]{:S(2)}, u32[]{:S(2)}) %all-to-all-start) | async-done | bytes 983072 | tf_op jit(solution)/shard_map/all_to_all | solution.py:58
  156.3 6.1 %all-to-all-start.1 = ((bf16[4,20,768]{2,1,0:T(8,128)(2,1)}), bf16[4,20,768]{2,1,0:T(8,128)(2,1)S(1)}, u32[]{:S(2)}, u32[]{:S(2)}) async-start(bf16[4,20,768]{2,1,0:T(8,128)(2,1)} %reshape.34), calls=%async_computation.1 | async-start | bytes 294912 | tf_op jit(solution)/shard_map/all_to_all | solution.py:60
  162.4 3.7 %all-to-all-done.1 = bf16[4,20,768]{2,1,0:T(8,128)(2,1)S(1)} async-done(((bf16[4,20,768]{2,1,0:T(8,128)(2,1)}), bf16[4,20,768]{2,1,0:T(8,128)(2,1)S(1)}, u32[]{:S(2)}, u32[]{:S(2)}) %all-to-all-start.1) | async-done | bytes 122912 | tf_op jit(solution)/shard_map/all_to_all | solution.py:60
  167.6 1.6 copy.14
  (34 shorter events, 3.6 us)
Async XLA Ops:
  0.6 6.6 %collective-permute-start = (bf16[80,384]{1,0:T(8,128)(2,1)}, bf16[80,384]{1,0:T(8,128)(2,1)S(1)}, u32[]{:S(2)}, u32[]{:S(2)}) collective-permute-start(bf16[80,384]{1,0:T(8,128)(2,1)} %param.4), channel_id=1, source_target_pairs={{0,8},{8,0},{1,9},{9,1},{2,10},{10,2},{3,11},{11,3},{4,12},{12,4},... | collective-permute-start | bytes 184328 | tf_op jit(solution)/shard_map/ppermute | solution.py:11
  7.3 25.0 %collective-permute-start.3 = (bf16[80,768]{1,0:T(8,128)(2,1)S(1)}, bf16[80,768]{1,0:T(8,128)(2,1)S(1)}, u32[]{:S(2)}, u32[]{:S(2)}) collective-permute-start(bf16[80,768]{1,0:T(8,128)(2,1)S(1)} %get-tuple-element.11), channel_id=1, source_target_pairs={{0,16},{16,32},{32,48},{48,0},{1,17},{17,33},{33,49},{49,1},{2,18}... | collective-permute-start | bytes 368648 | tf_op jit(solution)/shard_map/ppermute | solution.py:16
  13.1 19.2 %collective-permute-start.2 = (bf16[80,768]{1,0:T(8,128)(2,1)S(1)}, bf16[80,768]{1,0:T(8,128)(2,1)S(1)}, u32[]{:S(2)}, u32[]{:S(2)}) collective-permute-start(bf16[80,768]{1,0:T(8,128)(2,1)S(1)} %get-tuple-element.11), channel_id=1, source_target_pairs={{0,32},{16,48},{32,0},{48,16},{1,33},{17,49},{33,1},{49,17},{2,34}... | collective-permute-start | bytes 368648 | tf_op jit(solution)/shard_map/ppermute | solution.py:16
  21.3 12.3 %collective-permute-start.1 = (bf16[80,768]{1,0:T(8,128)(2,1)S(1)}, bf16[80,768]{1,0:T(8,128)(2,1)S(1)}, u32[]{:S(2)}, u32[]{:S(2)}) collective-permute-start(bf16[80,768]{1,0:T(8,128)(2,1)S(1)} %get-tuple-element.11), channel_id=1, source_target_pairs={{0,48},{16,0},{32,16},{48,32},{1,49},{17,1},{33,17},{49,33},{2,50}... | collective-permute-start | bytes 368648 | tf_op jit(solution)/shard_map/ppermute | solution.py:16
  26.4 10.2 %all-to-all-start.2 = ((bf16[4,20,768]{2,1,0:T(8,128)(2,1)}), bf16[4,20,768]{2,1,0:T(8,128)(2,1)S(1)}, u32[]{:S(2)}, u32[]{:S(2)}) async-start(bf16[4,20,768]{2,1,0:T(8,128)(2,1)} %bitcast.44), calls=%async_computation.2 | async-start | bytes 294912 | tf_op jit(solution)/shard_map/all_to_all | solution.py:38
  33.6 10.9 %collective-permute-start.4 = (bf16[320,768]{1,0:T(8,128)(2,1)S(1)}, bf16[320,768]{1,0:T(8,128)(2,1)S(1)}, u32[]{:S(2)}, u32[]{:S(2)}) collective-permute-start(bf16[320,768]{1,0:T(8,128)(2,1)S(1)} %pad_maximum_fusion.1), channel_id=1, source_target_pairs={{0,64},{64,0},{1,65},{65,1},{2,66},{66,2},{3,67},{67,3},{4,68},{68... | collective-permute-start | bytes 1474568 | tf_op jit(solution)/shard_map/ppermute | solution.py:11
  37.6 34.6 %all-to-all-start.3 = ((bf16[8,80,768]{2,1,0:T(8,128)(2,1)}), bf16[8,80,768]{2,1,0:T(8,128)(2,1)S(1)}, u32[]{:S(2)}, u32[]{:S(2)}) async-start(bf16[8,80,768]{2,1,0:T(8,128)(2,1)} %broadcast_in_dim.14), calls=%async_computation.3 | async-start | bytes 1966080 | tf_op jit(solution)/shard_map/all_to_all | solution.py:39
  74.7 11.2 %collective-permute-start.6 = (bf16[192,768]{1,0:T(8,128)(2,1)S(1)}, bf16[192,768]{1,0:T(8,128)(2,1)S(1)}, u32[]{:S(2)}, u32[]{:S(2)}) collective-permute-start(bf16[192,768]{1,0:T(8,128)(2,1)S(1)} %get-tuple-element.6), channel_id=1, source_target_pairs={{0,128},{128,256},{256,384},{384,0},{1,129},{129,257},{257,385},{3... | collective-permute-start | bytes 884744 | tf_op jit(solution)/shard_map/ppermute | solution.py:16
  77.8 9.6 %collective-permute-start.8 = (bf16[192,768]{1,0:T(8,128)(2,1)S(1)}, bf16[192,768]{1,0:T(8,128)(2,1)S(1)}, u32[]{:S(2)}, u32[]{:S(2)}) collective-permute-start(bf16[192,768]{1,0:T(8,128)(2,1)S(1)} %get-tuple-element.7), channel_id=1, source_target_pairs={{0,384},{128,0},{256,128},{384,256},{1,385},{129,1},{257,129},{385... | collective-permute-start | bytes 884744 | tf_op jit(solution)/shard_map/ppermute | solution.py:16
  81.2 11.8 %collective-permute-start.7 = (bf16[192,768]{1,0:T(8,128)(2,1)S(1)}, bf16[192,768]{1,0:T(8,128)(2,1)S(1)}, u32[]{:S(2)}, u32[]{:S(2)}) collective-permute-start(bf16[192,768]{1,0:T(8,128)(2,1)S(1)} %get-tuple-element.8), channel_id=1, source_target_pairs={{0,256},{128,384},{256,0},{384,128},{1,257},{129,385},{257,1},{385... | collective-permute-start | bytes 884744 | tf_op jit(solution)/shard_map/ppermute | solution.py:16
  93.3 5.7 %copy-start = (bf16[3072,384]{1,0:T(8,128)(2,1)S(1)}, bf16[3072,384]{1,0:T(8,128)(2,1)}, u32[]{:S(2)}) copy-start(bf16[3072,384]{1,0:T(8,128)(2,1)} %param.5) | copy-start | bytes 7077892
  94.4 32.1 %all-to-all-start.4 = ((bf16[8,192,384]{2,1,0:T(8,128)(2,1)}), bf16[8,192,384]{2,1,0:T(8,128)(2,1)S(1)}, u32[]{:S(2)}, u32[]{:S(2)}) async-start(bf16[8,192,384]{2,1,0:T(8,128)(2,1)} %bitcast.10), calls=%async_computation.4 | async-start | bytes 2359296 | tf_op jit(solution)/shard_map/all_to_all | solution.py:72
  99.0 25.6 %copy-start.1 = (bf16[640,768]{1,0:T(8,128)(2,1)S(1)}, bf16[640,768]{1,0:T(8,128)(2,1)}, u32[]{:S(2)}) copy-start(bf16[640,768]{1,0:T(8,128)(2,1)} %fusion.24) | copy-start | bytes 2949124
  99.1 25.4 %collective-permute-start.5 = (bf16[768,384]{1,0:T(8,128)(2,1)S(1)}, bf16[768,384]{1,0:T(8,128)(2,1)S(1)}, u32[]{:S(2)}, u32[]{:S(2)}) collective-permute-start(bf16[768,384]{1,0:T(8,128)(2,1)S(1)} %get-tuple-element.5), channel_id=1, source_target_pairs={{0,8},{8,0},{1,9},{9,1},{2,10},{10,2},{3,11},{11,3},{4,12},{12,4},... | collective-permute-start | bytes 1769480 | tf_op jit(solution)/shard_map/ppermute | solution.py:11
  126.5 29.0 %all-to-all-start = ((bf16[8,80,768]{2,1,0:T(8,128)(2,1)}), bf16[8,80,768]{2,1,0:T(8,128)(2,1)S(1)}, u32[]{:S(2)}, u32[]{:S(2)}) async-start(bf16[8,80,768]{2,1,0:T(8,128)(2,1)} %bitcast), calls=%async_computation | async-start | bytes 1966080 | tf_op jit(solution)/shard_map/all_to_all | solution.py:58
  130.2 36.8 %collective-permute-start.9 = (bf16[2,768,384]{2,1,0:T(8,128)(2,1)S(1)}, bf16[2,768,384]{2,1,0:T(8,128)(2,1)S(1)}, u32[]{:S(2)}, u32[]{:S(2)}) collective-permute-start(bf16[2,768,384]{2,1,0:T(8,128)(2,1)S(1)} %bitcast.45), channel_id=1, source_target_pairs={{0,64},{64,0},{1,65},{65,1},{2,66},{66,2},{3,67},{67,3},{4,68},{68... | collective-permute-start | bytes 3538952 | tf_op jit(solution)/shard_map/ppermute | solution.py:11
  156.3 9.9 %all-to-all-start.1 = ((bf16[4,20,768]{2,1,0:T(8,128)(2,1)}), bf16[4,20,768]{2,1,0:T(8,128)(2,1)S(1)}, u32[]{:S(2)}, u32[]{:S(2)}) async-start(bf16[4,20,768]{2,1,0:T(8,128)(2,1)} %reshape.34), calls=%async_computation.1 | async-start | bytes 294912 | tf_op jit(solution)/shard_map/all_to_all | solution.py:60

commit v2 on v1

v2 whole, which is shorter than its diff:
```python
import jax
import jax.numpy as jnp
from jax import lax
from jax.experimental import pallas as pl
from jax.experimental.pallas import tpu as pltpu
from jax.sharding import Mesh, PartitionSpec as P

F32 = jnp.float32
BF16 = jnp.bfloat16
I32 = jnp.int32
UNIT = 20
ROWS = 4 * UNIT
QUARTER = 768


def swap(value, axis):
    return lax.ppermute(value, axis, [(0, 1), (1, 0)])


def around(value, axis, step):
    size = lax.axis_size(axis)
    return lax.ppermute(value, axis, [(i, (i + step) % size) for i in range(size)])


def after(value, *others):
    return lax.optimization_barrier((value,) + others)[0]


def block(array, index, size):
    return lax.dynamic_slice_in_dim(array, index * size, size, 0)


def order_kernel(own, other, weight_own, weight_other, grads, parts, gathered, pick):
    core, zh = lax.axis_index("core"), lax.axis_index("zh")
    half = own.shape[0]
    total = 2 * half
    gathered[:half] = own[...]
    gathered[half:] = other[...]
    row = lax.broadcasted_iota(I32, (ROWS, 1), 0)
    unit = sum((row >= UNIT * i).astype(I32) for i in (1, 2, 3))
    zl = (unit >= 2).astype(I32)
    group = unit - 2 * zl
    side = jnp.where(group == core, 0, half)
    column = lax.broadcasted_iota(I32, (ROWS, total), 1)
    for y in range(8):
        piece = (2 * zl + (y // 4) - zh + 4) & 3
        source = side + piece * ROWS + (y % 4) * UNIT + row - unit * UNIT
        pick[y * ROWS : (y + 1) * ROWS] = jnp.where(source == column, 1.0, 0.0).astype(BF16)

    @pl.loop(0, total // 160)
    def _(tile):
        rows = pl.ds(pl.multiple_of(tile * 160, 160), 160)
        ordered = jnp.dot(pick[rows], gathered[...], preferred_element_type=F32).astype(BF16)
        grads[rows] = ordered
        wide = ordered.shape[1] // 2
        contract = (((1,), (1,)), ((), ()))
        parts[rows] = (
            lax.dot_general(ordered[:, :wide], weight_own[...], contract, preferred_element_type=F32)
            + lax.dot_general(ordered[:, wide:], weight_other[...], contract, preferred_element_type=F32)
        ).astype(BF16)


def order_and_multiply(own, other, weight_own, weight_other):
    half, columns = own.shape
    full = jax.ShapeDtypeStruct((2 * half, columns), BF16)
    spec = pl.BlockSpec(memory_space=pltpu.VMEM)
    return pl.pallas_call(
        order_kernel,
        out_shape=(full, full),
        in_specs=[spec] * 4,
        out_specs=(spec, spec),
        scratch_shapes=[pltpu.VMEM((2 * half, columns), BF16), pltpu.VMEM((2 * half, 2 * half), BF16)],
        compiler_params=pltpu.CompilerParams(vmem_limit_bytes=24 * 2**20),
        cost_estimate=pl.CostEstimate(flops=1000, bytes_accessed=1000, transcendentals=0),
        name="order_and_multiply",
    )(own, other, weight_own, weight_other)


def body(activations, out_grad, qkv_weight):
    x, core, zh, zl = (lax.axis_index(name) for name in ("x", "core", "zh", "zl"))
    ny = lax.axis_size("y")
    near = jnp.concatenate([out_grad] + [around(out_grad, "zh", -k) for k in (1, 2, 3)], axis=0)
    quarters = activations.reshape(UNIT, 4, QUARTER).transpose(1, 0, 2)
    mine = lax.all_to_all(quarters, ("zl", "core"), 0, 0, tiled=True).reshape(ROWS, QUARTER)
    spread = after(jnp.broadcast_to(mine[None], (ny, ROWS, QUARTER)), near)
    acts = lax.all_to_all(spread, "y", 0, 0, tiled=True).reshape(ny * ROWS, QUARTER)
    grads = jnp.concatenate([near, swap(near, "zl")], axis=1)
    weight_own = block(qkv_weight, zl * 2 + core, QUARTER)
    weight_other = block(qkv_weight, (1 - zl) * 2 + core, QUARTER)
    weight_other = swap(after(weight_other, grads), "zl")
    grads, parts = order_and_multiply(grads, swap(grads, "core"), weight_own, weight_other)
    acts, grads = lax.optimization_barrier((acts, grads, parts))[:2]
    parts = lax.all_to_all(parts.reshape(ny, ROWS, QUARTER), "y", 0, 0, tiled=True)
    parts = parts.astype(F32).sum(0).astype(BF16).reshape(4, UNIT, QUARTER)
    group = lax.dot_general(
        acts, grads, (((0,), (0,)), ((), ())), preferred_element_type=F32
    ).astype(BF16)
    total = block(group, x, 192).astype(F32)
    for k in (1, 2, 3):
        total += around(block(group, (x + k) % 4, 192), "x", k).astype(F32)
    total = (total / 8).astype(BF16)
    own, other = total[:, :384], swap(total[:, 384:], "zl")
    pair = jnp.stack([jnp.where(zl == 0, own, other), jnp.where(zl == 0, other, own)])
    spread = jnp.broadcast_to(pair[None], (4, 2, 192, 384))
    half = lax.all_to_all(after(spread, parts), "x", 0, 0, tiled=True)
    half = half.transpose(1, 0, 2, 3).reshape(2, 768, 384)
    place = zl * 2 + core

    def piece(q):
        return lax.dynamic_index_in_dim(parts, q, 0, keepdims=False)

    relative = [
        piece(place),
        swap(piece(place ^ 1), "core"),
        swap(piece(place ^ 2), "zl"),
        lax.ppermute(piece(place ^ 3), ("core", "zl"), [(0, 3), (3, 0), (1, 2), (2, 1)]),
    ]
    relative = jnp.stack(relative)
    input_grad = jnp.concatenate(
        [lax.dynamic_index_in_dim(relative, place ^ q, 0, keepdims=False) for q in range(4)], axis=1
    )
    half = after(half, input_grad)
    other_half = swap(half, "core")
    first = jnp.where(core == 0, half, other_half)
    second = jnp.where(core == 0, other_half, half)
    weight_grad = jnp.stack([first, second], axis=1).reshape(3072, 384)
    return input_grad, weight_grad


def solution(mesh):
    fine = Mesh(mesh.devices.reshape(4, 2, 4, 2, 8), ("x", "core", "zh", "zl", "y"))
    tokens, features = P(("x", "core", "zl", "y"), "zh"), P("zh", ("zl", "y"))
    return jax.shard_map(
        body,
        mesh=fine,
        in_specs=(tokens, P(("x", "core", "zh"), ("zl", "y")), features),
        out_specs=(tokens, features),
        check_vma=False,
    )
```

time: 170 us -> 128 us (0.75)
  waiting for transfers between devices: 80.2 us -> 30.7 us
  starting transfers between devices: 70.5 us -> 77.6 us
  matrix products: 8.33 us -> 2.32 us
  Pallas kernels: 0 us -> 5.13 us
    all_to_all x5 -> x4, waiting for transfers between devices: 47.7 us -> 3.02 us  [the longest x1 2.81 us: body(): lax.all_to_all(quarters, ('zl', 'core'), 0, 0, tiled=True)]
    ppermute x4 -> x7, starting transfers between devices: 16.1 us -> 25.4 us  [swap(): return lax.ppermute(value, axis, [(0, 1), (1, 0)])]
    dot_general x2 -> x0, matrix products: 5.99 us -> none  [the longest x1 4.05 us: body(): lax.dot_general(token_order(640, zh, core), grads, (((1,), (0,)), ((), ()...]
    ppermute x4 -> x7, waiting for transfers between devices: 22.9 us -> 17.3 us  [swap(): return lax.ppermute(value, axis, [(0, 1), (1, 0)])]
    pallas_call x0 -> x1, Pallas kernels: none -> 5.13 us  [order_and_multiply(): pl.pallas_call(order_kernel, out_shape=(full, full), in_specs=[spec] * 4,...]
    all_to_all x5 -> x4, starting transfers between devices: 27.1 us -> 22.1 us  [the longest x1 6.82 us: body(): lax.all_to_all(spread, 'y', 0, 0, tiled=True).reshape(ny * ROWS, QUARTER)]
    ppermute x0 -> x1, waiting for transfers between devices: none -> 3.04 us  [body(): lax.ppermute(piece(place ^ 3), ('core', 'zl'), [(0, 3), (3, 0), (1, 2), (...]
    ppermute x0 -> x1, starting transfers between devices: none -> 2.51 us  [body(): lax.ppermute(piece(place ^ 3), ('core', 'zl'), [(0, 3), (3, 0), (1, 2), (...]
  transfers between devices with their start and end apart: 15 -> 18, of which waited for: 9 -> 10; matrix products, arithmetic and copies ran while one was open for 7% -> 7% of each run, Pallas kernels for 0% -> 4%
where the time goes in v2:
time: 128 us; the launch traced here: 127 us
  starting transfers between devices  77.6 us (61%)
  waiting for transfers between devices  30.7 us (24%)
  local copies, waits for them, and re-layouts  8 us (6%)
  Pallas kernels  5.13 us (4%)
  other arithmetic  2.66 us (2%)
  matrix products  2.32 us (2%)
    ppermute x6, starting transfers between devices, around(): lax.ppermute(value, axis, [(i, (i + step) % size) for i in range(size)])  27.6 us
    ppermute x7, starting transfers between devices, swap(): return lax.ppermute(value, axis, [(0, 1), (1, 0)])  25.4 us
    ppermute x7, waiting for transfers between devices, swap(): return lax.ppermute(value, axis, [(0, 1), (1, 0)])  17.3 us
    ppermute x6, waiting for transfers between devices, around(): lax.ppermute(value, axis, [(i, (i + step) % size) for i in range(size)])  7.37 us
    all_to_all x1, starting transfers between devices, body(): lax.all_to_all(spread, 'y', 0, 0, tiled=True).reshape(ny * ROWS, QUARTER)  6.82 us
    all_to_all x1, starting transfers between devices, body(): lax.all_to_all(parts.reshape(ny, ROWS, QUARTER), 'y', 0, 0, tiled=True)  5.88 us
    pallas_call x1, Pallas kernels, order_and_multiply(): pl.pallas_call(order_kernel, out_shape=(full, full), in_specs=[spec] * 4,...  5.13 us
    all_to_all x1, starting transfers between devices, body(): lax.all_to_all(quarters, ('zl', 'core'), 0, 0, tiled=True)  4.82 us
  transfers between devices with their start and end apart: 18, of which 10 were waited for; matrix products, arithmetic and copies ran while one was open for 7% of the time, Pallas kernels for 4%

profile of v2, /device:TPU:1, one launch (start us, length us, event | category | flops | bytes accessed | tf_op | source)
XLA Modules:
  0.0 127.3 jit_solution(10434093612822367581)
XLA Ops:
  0.6 11.5 %collective-permute-start = (bf16[80,384]{1,0:T(8,128)(2,1)}, bf16[80,384]{1,0:T(8,128)(2,1)S(1)}, u32[]{:S(2)}, u32[]{:S(2)}) collective-permute-start(bf16[80,384]{1,0:T(8,128)(2,1)} %param.4), channel_id=1, source_target_pairs={{0,48},{16,0},{32,16},{48,32},{1,49},{17,1},{33,17},{49,33},{2,50}... | collective-permute-start | bytes 184328 | tf_op jit(solution)/shard_map/ppermute | solution.py:22
  12.1 1.9 %collective-permute-start.1 = (bf16[80,384]{1,0:T(8,128)(2,1)}, bf16[80,384]{1,0:T(8,128)(2,1)S(1)}, u32[]{:S(2)}, u32[]{:S(2)}) collective-permute-start(bf16[80,384]{1,0:T(8,128)(2,1)} %param.4), channel_id=1, source_target_pairs={{0,32},{16,48},{32,0},{48,16},{1,33},{17,49},{33,1},{49,17},{2,34}... | collective-permute-start | bytes 184328 | tf_op jit(solution)/shard_map/ppermute | solution.py:22
  14.1 4.2 %collective-permute-start.2 = (bf16[80,384]{1,0:T(8,128)(2,1)}, bf16[80,384]{1,0:T(8,128)(2,1)S(1)}, u32[]{:S(2)}, u32[]{:S(2)}) collective-permute-start(bf16[80,384]{1,0:T(8,128)(2,1)} %param.4), channel_id=1, source_target_pairs={{0,16},{16,32},{32,48},{48,0},{1,17},{17,33},{33,49},{49,1},{2,18}... | collective-permute-start | bytes 184328 | tf_op jit(solution)/shard_map/ppermute | solution.py:22
  20.0 4.8 %all-to-all-start.1 = ((bf16[4,20,768]{2,1,0:T(8,128)(2,1)}), bf16[4,20,768]{2,1,0:T(8,128)(2,1)S(1)}, u32[]{:S(2)}, u32[]{:S(2)}) async-start(bf16[4,20,768]{2,1,0:T(8,128)(2,1)} %bitcast.35), calls=%async_computation.1 | async-start | bytes 294912 | tf_op jit(solution)/shard_map/all_to_all | solution.py:84
  25.7 2.8 %all-to-all-done.1 = bf16[4,20,768]{2,1,0:T(8,128)(2,1)S(1)} async-done(((bf16[4,20,768]{2,1,0:T(8,128)(2,1)}), bf16[4,20,768]{2,1,0:T(8,128)(2,1)S(1)}, u32[]{:S(2)}, u32[]{:S(2)}) %all-to-all-start.1) | async-done | bytes 122912 | tf_op jit(solution)/shard_map/all_to_all | solution.py:84
  29.6 6.8 %all-to-all-start.2 = ((bf16[8,80,768]{2,1,0:T(8,128)(2,1)}), bf16[8,80,768]{2,1,0:T(8,128)(2,1)S(1)}, u32[]{:S(2)}, u32[]{:S(2)}) async-start(bf16[8,80,768]{2,1,0:T(8,128)(2,1)} %broadcast_in_dim.14), calls=%async_computation.2 | async-start | bytes 1966080 | tf_op jit(solution)/shard_map/all_to_all | solution.py:86
  36.4 2.5 %collective-permute-start.3 = (bf16[320,384]{1,0:T(8,128)(2,1)S(1)}, bf16[320,384]{1,0:T(8,128)(2,1)S(1)}, u32[]{:S(2)}, u32[]{:S(2)}) collective-permute-start(bf16[320,384]{1,0:T(8,128)(2,1)S(1)} %constant_dynamic-update-slice_fusion), channel_id=1, source_target_pairs={{0,8},{8,0},{1,9},{9,1},{2,10},{10,2},{3,11},{11,3},{4,12},{12,4},... | collective-permute-start | bytes 737288 | tf_op jit(solution)/shard_map/ppermute | solution.py:17
  38.9 1.4 %constant_dynamic-slice_fusion.4 = (bf16[768,384]{1,0:T(8,128)(2,1)S(1)}, bf16[768,384]{1,0:T(8,128)(2,1)S(1)}) fusion(bf16[3072,384]{1,0:T(8,128)(2,1)} %param.5, s32[]{:T(128)S(6)} %select_n.75, s32[]{:T(128)S(6)} %select_n.74), kind=kLoop, calls=%fused_computation.27 | loop fusion | bytes 2359304 | tf_op jit(solution)/shard_map/dynamic_slice | solution.py:30
  40.2 4.1 %collective-permute-done.3 = bf16[320,384]{1,0:T(8,128)(2,1)S(1)} collective-permute-done((bf16[320,384]{1,0:T(8,128)(2,1)S(1)}, bf16[320,384]{1,0:T(8,128)(2,1)S(1)}, u32[]{:S(2)}, u32[]{:S(2)}) %collective-permute-start.3) | collective-permute-done | bytes 245792 | tf_op jit(solution)/shard_map/ppermute | solution.py:17
  44.4 3.0 %collective-permute-start.5 = (bf16[768,384]{1,0:T(8,128)(2,1)S(1)}, bf16[768,384]{1,0:T(8,128)(2,1)S(1)}, u32[]{:S(2)}, u32[]{:S(2)}) collective-permute-start(bf16[768,384]{1,0:T(8,128)(2,1)S(1)} %get-tuple-element.10), channel_id=1, source_target_pairs={{0,8},{8,0},{1,9},{9,1},{2,10},{10,2},{3,11},{11,3},{4,12},{12,4},... | collective-permute-start | bytes 1769480 | tf_op jit(solution)/shard_map/ppermute | solution.py:17
  47.4 4.0 %collective-permute-start.4 = (bf16[320,768]{1,0:T(8,128)(2,1)S(1)}, bf16[320,768]{1,0:T(8,128)(2,1)S(1)}, u32[]{:S(2)}, u32[]{:S(2)}) collective-permute-start(bf16[320,768]{1,0:T(8,128)(2,1)S(1)} %pad_maximum_fusion.1.own), channel_id=1, source_target_pairs={{0,64},{64,0},{1,65},{65,1},{2,66},{66,2},{3,67},{67,3},{4,68},{68... | collective-permute-start | bytes 1474568 | tf_op jit(solution)/shard_map/ppermute | solution.py:17
  51.4 1.5 %collective-permute-done.4.other = bf16[320,768]{1,0:T(8,128)(2,1)S(1)} collective-permute-done((bf16[320,768]{1,0:T(8,128)(2,1)S(1)}, bf16[320,768]{1,0:T(8,128)(2,1)S(1)}, u32[]{:S(2)}, u32[]{:S(2)}) %collective-permute-start.4) | collective-permute-done | bytes 491552 | tf_op jit(solution)/shard_map/ppermute | solution.py:17
  52.8 6.0 %collective-permute-done.5.weight_other = bf16[768,384]{1,0:T(8,128)(2,1)S(1)} collective-permute-done((bf16[768,384]{1,0:T(8,128)(2,1)S(1)}, bf16[768,384]{1,0:T(8,128)(2,1)S(1)}, u32[]{:S(2)}, u32[]{:S(2)}) %collective-permute-start.5) | collective-permute-done | bytes 589856 | tf_op jit(solution)/shard_map/ppermute | solution.py:17
  58.8 5.1 %order_and_multiply.1 = (bf16[640,768]{1,0:T(8,128)(2,1)S(1)}, bf16[640,768]{1,0:T(8,128)(2,1)}) custom-call(bf16[320,768]{1,0:T(8,128)(2,1)S(1)} %pad_maximum_fusion.1.own, bf16[320,768]{1,0:T(8,128)(2,1)S(1)} %collective-permute-done.4.other, bf16[768,384]{1,0:T(8,128)(2,1)S(1)} %get-tuple-element.21.weight_own, ...), custom_call_target="tpu_custom_call" | custom-call | flops 1000 | bytes 1000 | tf_op jit(solution)/shard_map/order_and_multiply/pallas_call | solution.py:67
  64.2 5.9 %all-to-all-start = ((bf16[8,80,768]{2,1,0:T(8,128)(2,1)}), bf16[8,80,768]{2,1,0:T(8,128)(2,1)S(1)}, u32[]{:S(2)}, u32[]{:S(2)}) async-start(bf16[8,80,768]{2,1,0:T(8,128)(2,1)} %bitcast), calls=%async_computation | async-start | bytes 1966080 | tf_op jit(solution)/shard_map/all_to_all | solution.py:93
  70.1 2.3 %convolution_convert_fusion = bf16[768,768]{1,0:T(8,128)(2,1)S(1)} fusion(bf16[640,768]{1,0:T(8,128)(2,1)} %bitcast.39, bf16[640,768]{1,0:T(8,128)(2,1)S(1)} %get-tuple-element.15), kind=kOutput, calls=%fused_computation.1 | convolution fusion | flops 755564544 | bytes 3145728 | tf_op jit(solution)/shard_map/dot_general | solution.py:95
  72.5 4.7 %collective-permute-start.10 = (bf16[192,768]{1,0:T(8,128)(2,1)S(1)}, bf16[192,768]{1,0:T(8,128)(2,1)S(1)}, u32[]{:S(2)}, u32[]{:S(2)}) collective-permute-start(bf16[192,768]{1,0:T(8,128)(2,1)S(1)} %get-tuple-element.24), channel_id=1, source_target_pairs={{0,256},{128,384},{256,0},{384,128},{1,257},{129,385},{257,1},{385... | collective-permute-start | bytes 884744 | tf_op jit(solution)/shard_map/ppermute | solution.py:22
  77.1 2.8 %collective-permute-start.11 = (bf16[192,768]{1,0:T(8,128)(2,1)S(1)}, bf16[192,768]{1,0:T(8,128)(2,1)}, u32[]{:S(2)}, u32[]{:S(2)}) collective-permute-start(bf16[192,768]{1,0:T(8,128)(2,1)S(1)} %get-tuple-element.23), channel_id=1, source_target_pairs={{0,384},{128,0},{256,128},{384,256},{1,385},{129,1},{257,129},{385... | collective-permute-start | bytes 884744 | tf_op jit(solution)/shard_map/ppermute | solution.py:22
  79.9 2.5 %collective-permute-start.9 = (bf16[192,768]{1,0:T(8,128)(2,1)S(1)}, bf16[192,768]{1,0:T(8,128)(2,1)}, u32[]{:S(2)}, u32[]{:S(2)}) collective-permute-start(bf16[192,768]{1,0:T(8,128)(2,1)S(1)} %get-tuple-element.22), channel_id=1, source_target_pairs={{0,128},{128,256},{256,384},{384,0},{1,129},{129,257},{257,385},{3... | collective-permute-start | bytes 884744 | tf_op jit(solution)/shard_map/ppermute | solution.py:22
  82.5 5.0 %collective-permute-done.11 = bf16[192,768]{1,0:T(8,128)(2,1)} collective-permute-done((bf16[192,768]{1,0:T(8,128)(2,1)S(1)}, bf16[192,768]{1,0:T(8,128)(2,1)}, u32[]{:S(2)}, u32[]{:S(2)}) %collective-permute-start.11) | collective-permute-done | bytes 294944 | tf_op jit(solution)/shard_map/ppermute | solution.py:22
  87.5 2.3 %collective-permute-done.9 = bf16[192,768]{1,0:T(8,128)(2,1)} collective-permute-done((bf16[192,768]{1,0:T(8,128)(2,1)S(1)}, bf16[192,768]{1,0:T(8,128)(2,1)}, u32[]{:S(2)}, u32[]{:S(2)}) %collective-permute-start.9) | collective-permute-done | bytes 294944 | tf_op jit(solution)/shard_map/ppermute | solution.py:22
  89.8 1.2 multiply_convert_fusion
  91.1 2.9 %collective-permute-start.12 = (bf16[192,384]{1,0:T(8,128)(2,1)S(1)}, bf16[192,384]{1,0:T(8,128)(2,1)S(1)}, u32[]{:S(2)}, u32[]{:S(2)}) collective-permute-start(bf16[192,384]{1,0:T(8,128)(2,1)S(1)} %slice.9), channel_id=1, source_target_pairs={{0,8},{8,0},{1,9},{9,1},{2,10},{10,2},{3,11},{11,3},{4,12},{12,4},... | collective-permute-start | bytes 442376 | tf_op jit(solution)/shard_map/ppermute | solution.py:17
  94.0 3.2 %collective-permute-done.12 = bf16[192,384]{1,0:T(8,128)(2,1)S(1)} collective-permute-done((bf16[192,384]{1,0:T(8,128)(2,1)S(1)}, bf16[192,384]{1,0:T(8,128)(2,1)S(1)}, u32[]{:S(2)}, u32[]{:S(2)}) %collective-permute-start.12) | collective-permute-done | bytes 147488 | tf_op jit(solution)/shard_map/ppermute | solution.py:17
  98.6 4.6 %all-to-all-start.3 = ((bf16[4,2,192,384]{3,2,1,0:T(8,128)(2,1)}), bf16[4,2,192,384]{3,2,1,0:T(8,128)(2,1)S(1)}, u32[]{:S(2)}, u32[]{:S(2)}) async-start(bf16[4,2,192,384]{3,2,1,0:T(8,128)(2,1)} %broadcast_in_dim.15), calls=%async_computation.3 | async-start | bytes 2359296 | tf_op jit(solution)/shard_map/all_to_all | solution.py:105
  103.2 6.1 %collective-permute-start.6 = (bf16[20,768]{1,0:T(8,128)(2,1)S(1)}, bf16[20,768]{1,0:T(8,128)(2,1)S(1)}, u32[]{:S(2)}, u32[]{:S(2)}) collective-permute-start(bf16[20,768]{1,0:T(8,128)(2,1)S(1)} %get-tuple-element.34), channel_id=1, source_target_pairs={{0,64},{64,0},{1,65},{65,1},{2,66},{66,2},{3,67},{67,3},{4,68},{68... | collective-permute-start | bytes 92168 | tf_op jit(solution)/shard_map/ppermute | solution.py:17
  109.4 3.0 %collective-permute-start.7 = (bf16[20,768]{1,0:T(8,128)(2,1)S(1)}, bf16[20,768]{1,0:T(8,128)(2,1)S(1)}, u32[]{:S(2)}, u32[]{:S(2)}) collective-permute-start(bf16[20,768]{1,0:T(8,128)(2,1)S(1)} %get-tuple-element.33), channel_id=1, source_target_pairs={{0,8},{8,0},{1,9},{9,1},{2,10},{10,2},{3,11},{11,3},{4,12},{12,4},... | collective-permute-start | bytes 92168 | tf_op jit(solution)/shard_map/ppermute | solution.py:17
  112.3 2.5 %collective-permute-start.8 = (bf16[20,768]{1,0:T(8,128)(2,1)S(1)}, bf16[20,768]{1,0:T(8,128)(2,1)S(1)}, u32[]{:S(2)}, u32[]{:S(2)}) collective-permute-start(bf16[20,768]{1,0:T(8,128)(2,1)S(1)} %get-tuple-element.32), channel_id=1, source_target_pairs={{0,72},{72,0},{8,64},{64,8},{1,73},{73,1},{9,65},{65,9},{2,74},{74... | collective-permute-start | bytes 92168 | tf_op jit(solution)/shard_map/ppermute | solution.py:116
  114.9 3.0 %collective-permute-done.8 = bf16[20,768]{1,0:T(8,128)(2,1)S(1)} collective-permute-done((bf16[20,768]{1,0:T(8,128)(2,1)S(1)}, bf16[20,768]{1,0:T(8,128)(2,1)S(1)}, u32[]{:S(2)}, u32[]{:S(2)}) %collective-permute-start.8) | collective-permute-done | bytes 30752 | tf_op jit(solution)/shard_map/ppermute | solution.py:116
  118.8 3.9 %collective-permute-start.13 = (bf16[2,768,384]{2,1,0:T(8,128)(2,1)S(1)}, bf16[2,768,384]{2,1,0:T(8,128)(2,1)S(1)}, u32[]{:S(2)}, u32[]{:S(2)}) collective-permute-start(bf16[2,768,384]{2,1,0:T(8,128)(2,1)S(1)} %bitcast.36), channel_id=1, source_target_pairs={{0,64},{64,0},{1,65},{65,1},{2,66},{66,2},{3,67},{67,3},{4,68},{68... | collective-permute-start | bytes 3538952 | tf_op jit(solution)/shard_map/ppermute | solution.py:17
  122.7 2.4 %collective-permute-done.13 = bf16[2,768,384]{2,1,0:T(8,128)(2,1)S(1)} collective-permute-done((bf16[2,768,384]{2,1,0:T(8,128)(2,1)S(1)}, bf16[2,768,384]{2,1,0:T(8,128)(2,1)S(1)}, u32[]{:S(2)}, u32[]{:S(2)}) %collective-permute-start.13) | collective-permute-done | bytes 1179680 | tf_op jit(solution)/shard_map/ppermute | solution.py:17
  125.7 1.6 %copy.14 = bf16[2,2,768,384]{3,2,1,0:T(8,128)(2,1)} copy(bf16[2,2,768,384]{3,2,0,1:T(8,128)(2,1)S(1)} %pad_maximum_fusion) | data formatting | bytes 4718592 | tf_op jit(solution)/shard_map/stack | solution.py:126
  (34 shorter events, 6.7 us)
Async XLA Ops:
  0.6 25.0 %collective-permute-start = (bf16[80,384]{1,0:T(8,128)(2,1)}, bf16[80,384]{1,0:T(8,128)(2,1)S(1)}, u32[]{:S(2)}, u32[]{:S(2)}) collective-permute-start(bf16[80,384]{1,0:T(8,128)(2,1)} %param.4), channel_id=1, source_target_pairs={{0,48},{16,0},{32,16},{48,32},{1,49},{17,1},{33,17},{49,33},{2,50}... | collective-permute-start | bytes 184328 | tf_op jit(solution)/shard_map/ppermute | solution.py:22
  12.1 13.5 %collective-permute-start.1 = (bf16[80,384]{1,0:T(8,128)(2,1)}, bf16[80,384]{1,0:T(8,128)(2,1)S(1)}, u32[]{:S(2)}, u32[]{:S(2)}) collective-permute-start(bf16[80,384]{1,0:T(8,128)(2,1)} %param.4), channel_id=1, source_target_pairs={{0,32},{16,48},{32,0},{48,16},{1,33},{17,49},{33,1},{49,17},{2,34}... | collective-permute-start | bytes 184328 | tf_op jit(solution)/shard_map/ppermute | solution.py:22
  14.1 11.6 %collective-permute-start.2 = (bf16[80,384]{1,0:T(8,128)(2,1)}, bf16[80,384]{1,0:T(8,128)(2,1)S(1)}, u32[]{:S(2)}, u32[]{:S(2)}) collective-permute-start(bf16[80,384]{1,0:T(8,128)(2,1)} %param.4), channel_id=1, source_target_pairs={{0,16},{16,32},{32,48},{48,0},{1,17},{17,33},{33,49},{49,1},{2,18}... | collective-permute-start | bytes 184328 | tf_op jit(solution)/shard_map/ppermute | solution.py:22
  20.0 8.5 %all-to-all-start.1 = ((bf16[4,20,768]{2,1,0:T(8,128)(2,1)}), bf16[4,20,768]{2,1,0:T(8,128)(2,1)S(1)}, u32[]{:S(2)}, u32[]{:S(2)}) async-start(bf16[4,20,768]{2,1,0:T(8,128)(2,1)} %bitcast.35), calls=%async_computation.1 | async-start | bytes 294912 | tf_op jit(solution)/shard_map/all_to_all | solution.py:84
  29.6 34.6 %all-to-all-start.2 = ((bf16[8,80,768]{2,1,0:T(8,128)(2,1)}), bf16[8,80,768]{2,1,0:T(8,128)(2,1)S(1)}, u32[]{:S(2)}, u32[]{:S(2)}) async-start(bf16[8,80,768]{2,1,0:T(8,128)(2,1)} %broadcast_in_dim.14), calls=%async_computation.2 | async-start | bytes 1966080 | tf_op jit(solution)/shard_map/all_to_all | solution.py:86
  36.4 8.0 %collective-permute-start.3 = (bf16[320,384]{1,0:T(8,128)(2,1)S(1)}, bf16[320,384]{1,0:T(8,128)(2,1)S(1)}, u32[]{:S(2)}, u32[]{:S(2)}) collective-permute-start(bf16[320,384]{1,0:T(8,128)(2,1)S(1)} %constant_dynamic-update-slice_fusion), channel_id=1, source_target_pairs={{0,8},{8,0},{1,9},{9,1},{2,10},{10,2},{3,11},{11,3},{4,12},{12,4},... | collective-permute-start | bytes 737288 | tf_op jit(solution)/shard_map/ppermute | solution.py:17
  44.4 14.4 %collective-permute-start.5 = (bf16[768,384]{1,0:T(8,128)(2,1)S(1)}, bf16[768,384]{1,0:T(8,128)(2,1)S(1)}, u32[]{:S(2)}, u32[]{:S(2)}) collective-permute-start(bf16[768,384]{1,0:T(8,128)(2,1)S(1)} %get-tuple-element.10), channel_id=1, source_target_pairs={{0,8},{8,0},{1,9},{9,1},{2,10},{10,2},{3,11},{11,3},{4,12},{12,4},... | collective-permute-start | bytes 1769480 | tf_op jit(solution)/shard_map/ppermute | solution.py:17
  47.4 5.4 %collective-permute-start.4 = (bf16[320,768]{1,0:T(8,128)(2,1)S(1)}, bf16[320,768]{1,0:T(8,128)(2,1)S(1)}, u32[]{:S(2)}, u32[]{:S(2)}) collective-permute-start(bf16[320,768]{1,0:T(8,128)(2,1)S(1)} %pad_maximum_fusion.1.own), channel_id=1, source_target_pairs={{0,64},{64,0},{1,65},{65,1},{2,66},{66,2},{3,67},{67,3},{4,68},{68... | collective-permute-start | bytes 1474568 | tf_op jit(solution)/shard_map/ppermute | solution.py:17
  64.2 5.9 %copy-start = (bf16[8,80,768]{2,1,0:T(8,128)(2,1)}, bf16[8,80,768]{2,1,0:T(8,128)(2,1)S(1)}, u32[]{:S(2)}) copy-start(bf16[8,80,768]{2,1,0:T(8,128)(2,1)S(1)} %all-to-all-done.2) | copy-start | bytes 2949124
  64.2 33.1 %all-to-all-start = ((bf16[8,80,768]{2,1,0:T(8,128)(2,1)}), bf16[8,80,768]{2,1,0:T(8,128)(2,1)S(1)}, u32[]{:S(2)}, u32[]{:S(2)}) async-start(bf16[8,80,768]{2,1,0:T(8,128)(2,1)} %bitcast), calls=%async_computation | async-start | bytes 1966080 | tf_op jit(solution)/shard_map/all_to_all | solution.py:93
  72.5 10.0 %collective-permute-start.10 = (bf16[192,768]{1,0:T(8,128)(2,1)S(1)}, bf16[192,768]{1,0:T(8,128)(2,1)S(1)}, u32[]{:S(2)}, u32[]{:S(2)}) collective-permute-start(bf16[192,768]{1,0:T(8,128)(2,1)S(1)} %get-tuple-element.24), channel_id=1, source_target_pairs={{0,256},{128,384},{256,0},{384,128},{1,257},{129,385},{257,1},{385... | collective-permute-start | bytes 884744 | tf_op jit(solution)/shard_map/ppermute | solution.py:22
  77.1 10.3 %collective-permute-start.11 = (bf16[192,768]{1,0:T(8,128)(2,1)S(1)}, bf16[192,768]{1,0:T(8,128)(2,1)}, u32[]{:S(2)}, u32[]{:S(2)}) collective-permute-start(bf16[192,768]{1,0:T(8,128)(2,1)S(1)} %get-tuple-element.23), channel_id=1, source_target_pairs={{0,384},{128,0},{256,128},{384,256},{1,385},{129,1},{257,129},{385... | collective-permute-start | bytes 884744 | tf_op jit(solution)/shard_map/ppermute | solution.py:22
  79.9 9.9 %collective-permute-start.9 = (bf16[192,768]{1,0:T(8,128)(2,1)S(1)}, bf16[192,768]{1,0:T(8,128)(2,1)}, u32[]{:S(2)}, u32[]{:S(2)}) collective-permute-start(bf16[192,768]{1,0:T(8,128)(2,1)S(1)} %get-tuple-element.22), channel_id=1, source_target_pairs={{0,128},{128,256},{256,384},{384,0},{1,129},{129,257},{257,385},{3... | collective-permute-start | bytes 884744 | tf_op jit(solution)/shard_map/ppermute | solution.py:22
  91.1 6.2 %collective-permute-start.12 = (bf16[192,384]{1,0:T(8,128)(2,1)S(1)}, bf16[192,384]{1,0:T(8,128)(2,1)S(1)}, u32[]{:S(2)}, u32[]{:S(2)}) collective-permute-start(bf16[192,384]{1,0:T(8,128)(2,1)S(1)} %slice.9), channel_id=1, source_target_pairs={{0,8},{8,0},{1,9},{9,1},{2,10},{10,2},{3,11},{11,3},{4,12},{12,4},... | collective-permute-start | bytes 442376 | tf_op jit(solution)/shard_map/ppermute | solution.py:17
  98.6 20.0 %all-to-all-start.3 = ((bf16[4,2,192,384]{3,2,1,0:T(8,128)(2,1)}), bf16[4,2,192,384]{3,2,1,0:T(8,128)(2,1)S(1)}, u32[]{:S(2)}, u32[]{:S(2)}) async-start(bf16[4,2,192,384]{3,2,1,0:T(8,128)(2,1)} %broadcast_in_dim.15), calls=%async_computation.3 | async-start | bytes 2359296 | tf_op jit(solution)/shard_map/all_to_all | solution.py:105
  103.2 11.6 %collective-permute-start.6 = (bf16[20,768]{1,0:T(8,128)(2,1)S(1)}, bf16[20,768]{1,0:T(8,128)(2,1)S(1)}, u32[]{:S(2)}, u32[]{:S(2)}) collective-permute-start(bf16[20,768]{1,0:T(8,128)(2,1)S(1)} %get-tuple-element.34), channel_id=1, source_target_pairs={{0,64},{64,0},{1,65},{65,1},{2,66},{66,2},{3,67},{67,3},{4,68},{68... | collective-permute-start | bytes 92168 | tf_op jit(solution)/shard_map/ppermute | solution.py:17
  109.4 5.5 %collective-permute-start.7 = (bf16[20,768]{1,0:T(8,128)(2,1)S(1)}, bf16[20,768]{1,0:T(8,128)(2,1)S(1)}, u32[]{:S(2)}, u32[]{:S(2)}) collective-permute-start(bf16[20,768]{1,0:T(8,128)(2,1)S(1)} %get-tuple-element.33), channel_id=1, source_target_pairs={{0,8},{8,0},{1,9},{9,1},{2,10},{10,2},{3,11},{11,3},{4,12},{12,4},... | collective-permute-start | bytes 92168 | tf_op jit(solution)/shard_map/ppermute | solution.py:17
  112.3 5.6 %collective-permute-start.8 = (bf16[20,768]{1,0:T(8,128)(2,1)S(1)}, bf16[20,768]{1,0:T(8,128)(2,1)S(1)}, u32[]{:S(2)}, u32[]{:S(2)}) collective-permute-start(bf16[20,768]{1,0:T(8,128)(2,1)S(1)} %get-tuple-element.32), channel_id=1, source_target_pairs={{0,72},{72,0},{8,64},{64,8},{1,73},{73,1},{9,65},{65,9},{2,74},{74... | collective-permute-start | bytes 92168 | tf_op jit(solution)/shard_map/ppermute | solution.py:116
  118.8 6.4 %collective-permute-start.13 = (bf16[2,768,384]{2,1,0:T(8,128)(2,1)S(1)}, bf16[2,768,384]{2,1,0:T(8,128)(2,1)S(1)}, u32[]{:S(2)}, u32[]{:S(2)}) collective-permute-start(bf16[2,768,384]{2,1,0:T(8,128)(2,1)S(1)} %bitcast.36), channel_id=1, source_target_pairs={{0,64},{64,0},{1,65},{65,1},{2,66},{66,2},{3,67},{67,3},{4,68},{68... | collective-permute-start | bytes 3538952 | tf_op jit(solution)/shard_map/ppermute | solution.py:17

commit v3 on v0

v3 whole, which is shorter than its diff:
```python
import jax
import jax.numpy as jnp
from jax import lax
from jax.experimental import pallas as pl
from jax.experimental.pallas import tpu as pltpu
from jax.sharding import Mesh, PartitionSpec as P

F32 = jnp.float32
BF16 = jnp.bfloat16
I32 = jnp.int32
UNIT = 20
PAIR = 2 * UNIT


def swap(value, axis):
    return lax.ppermute(value, axis, [(0, 1), (1, 0)])


def around(value, axis, step):
    size = lax.axis_size(axis)
    return lax.ppermute(value, axis, [(i, (i + step) % size) for i in range(size)])


def after(value, *others):
    return lax.optimization_barrier((value,) + others)[0]


def block(array, index, size):
    return lax.dynamic_slice_in_dim(array, index * size, size, 0)


def call(kernel, out_shape, in_spaces, out_spaces, scratch, name, flops=1000):
    return pl.pallas_call(
        kernel,
        out_shape=out_shape,
        in_specs=[pl.BlockSpec(memory_space=space) for space in in_spaces],
        out_specs=jax.tree.map(lambda space: pl.BlockSpec(memory_space=space), out_spaces),
        scratch_shapes=scratch,
        compiler_params=pltpu.CompilerParams(vmem_limit_bytes=10 * 2**20),
        cost_estimate=pl.CostEstimate(flops=flops, bytes_accessed=1000, transcendentals=0),
        name=name,
    )


def spread_kernel(rows, gate, out):
    for y in range(out.shape[0]):
        out[y] = rows[...]


def spread_out(rows, gate):
    return call(
        spread_kernel,
        jax.ShapeDtypeStruct((8,) + rows.shape, BF16),
        [pltpu.VMEM, pl.ANY],
        pltpu.VMEM,
        [],
        "spread",
    )(rows, gate)


def order_kernel(piece0, piece1, piece2, piece3, grads, gathered, pick):
    zh = lax.axis_index("zh")
    total = grads.shape[0]
    quarter = total // 4
    for k, piece in enumerate((piece0, piece1, piece2, piece3)):
        gathered[k * quarter : (k + 1) * quarter] = piece[...]
    row = lax.broadcasted_iota(I32, (PAIR, 1), 0)
    zl = (row >= UNIT).astype(I32)
    column = lax.broadcasted_iota(I32, (PAIR, total), 1)
    for y in range(8):
        piece = (2 * zl + (y // 4) - zh + 4) & 3
        source = piece * quarter + (y % 4) * UNIT + row - zl * UNIT
        pick[y * PAIR : (y + 1) * PAIR] = jnp.where(source == column, 1.0, 0.0)
    grads[...] = jnp.dot(
        pick[...].astype(BF16), gathered[...], preferred_element_type=F32
    ).astype(BF16)


def order(pieces):
    rows, columns = pieces[0].shape
    return call(
        order_kernel,
        jax.ShapeDtypeStruct((4 * rows, columns), BF16),
        [pltpu.VMEM] * 4,
        pltpu.VMEM,
        [pltpu.VMEM((4 * rows, columns), BF16), pltpu.VMEM((4 * rows, 4 * rows), F32)],
        "order",
    )(*pieces)


def multiply_kernel(near, other, weight, received, gate, parts, held, sem):
    rows, columns = received.shape
    first = (lax.axis_index("zl") * 2 + lax.axis_index("core")) * rows
    copy = pltpu.make_async_copy(weight.at[pl.ds(pl.multiple_of(first, rows), rows)], held, sem)
    copy.start()
    copy.wait()
    contract = (((1,), (1,)), ((), ()))
    tokens = near.shape[0]
    for group, grads in enumerate((near, other)):
        for tile in range(rows // 256):
            inner = slice(tile * 256, (tile + 1) * 256)
            parts[group * tokens : (group + 1) * tokens, inner] = (
                lax.dot_general(
                    grads[:, :columns], held[inner], contract, preferred_element_type=F32
                )
                + lax.dot_general(
                    grads[:, columns:], received[inner], contract, preferred_element_type=F32
                )
            ).astype(BF16)


def multiply(near, other, weight, received, gate):
    return call(
        multiply_kernel,
        jax.ShapeDtypeStruct((2 * near.shape[0], received.shape[0]), BF16),
        [pltpu.VMEM, pltpu.VMEM, pl.ANY, pltpu.VMEM, pl.ANY],
        pltpu.VMEM,
        [pltpu.VMEM(received.shape, BF16), pltpu.SemaphoreType.DMA],
        "multiply",
        3 * 10**9,
    )(near, other, weight, received, gate)


def outer_kernel(acts, near, other, own, send1, send2, send3, total):
    rows = near.shape[0]
    width = near.shape[1] // 3
    for tile in range(3):
        columns = slice(tile * width, (tile + 1) * width)
        total[:, columns] = sum(
            lax.dot_general(
                acts[k * rows : (k + 1) * rows],
                grads[:, columns],
                (((0,), (0,)), ((), ())),
                preferred_element_type=F32,
            )
            for k, grads in enumerate((near, other))
        )
    chunk = own.shape[0]
    x = lax.axis_index("x")
    for k, out in enumerate((own, send1, send2, send3)):
        start = pl.multiple_of(((x + k) & 3) * chunk, chunk)
        out[...] = total[pl.ds(start, chunk)].astype(out.dtype)


def outer(acts, near, other):
    features, columns = acts.shape[1], near.shape[1]
    shape = (features // 4, columns)
    return call(
        outer_kernel,
        (jax.ShapeDtypeStruct(shape, F32),) + (jax.ShapeDtypeStruct(shape, BF16),) * 3,
        [pltpu.VMEM] * 3,
        (pltpu.VMEM,) * 4,
        [pltpu.VMEM((features, columns), F32)],
        "outer",
    )(acts, near, other)


def combine_kernel(own, got1, got2, got3, near, far):
    columns = near.shape[1]
    total = own[...] + got1[...].astype(F32) + got2[...].astype(F32) + got3[...].astype(F32)
    total = (total * 0.125).astype(BF16)
    near[...] = total[:, :columns]
    far[...] = total[:, columns:]


def combine(own, got):
    half = jax.ShapeDtypeStruct((own.shape[0], own.shape[1] // 2), BF16)
    return call(
        combine_kernel, (half, half), [pltpu.VMEM] * 4, (pltpu.VMEM, pltpu.VMEM), [], "combine", 10**11
    )(own, *got)


def add_up_kernel(source, gate, total, parts, sem):
    copy = pltpu.make_async_copy(source, parts, sem)
    copy.start()
    copy.wait()
    sums = parts[0].astype(F32)
    for y in range(1, parts.shape[0]):
        sums += parts[y].astype(F32)
    total[...] = sums.astype(BF16)


def add_up(parts, gate):
    return call(
        add_up_kernel,
        jax.ShapeDtypeStruct(parts.shape[1:], BF16),
        [pltpu.HBM, pl.ANY],
        pltpu.VMEM,
        [pltpu.VMEM(parts.shape, BF16), pltpu.SemaphoreType.DMA],
        "add_up",
    )(parts, gate)


def stack_kernel(piece0, piece1, piece2, piece3, gate, out):
    for k, piece in enumerate((piece0, piece1, piece2, piece3)):
        out[k] = piece[...]


def stack(pieces, gate):
    return call(
        stack_kernel,
        jax.ShapeDtypeStruct((4,) + pieces[0].shape, BF16),
        [pltpu.VMEM] * 4 + [pl.ANY],
        pltpu.VMEM,
        [],
        "stack",
    )(*pieces, gate)


def place_kernel(near, next1, next2, next3, other, out, sems):
    x, core = lax.axis_index("x"), lax.axis_index("core")
    chunk = near.shape[1]
    copies = []
    for k, mine in enumerate((near, next1, next2, next3)):
        for zl in range(2):
            for far in range(2):
                half = 1 - core if far else core
                row = (((zl * 2 + half) * 4) + ((x - k + 4) & 3)) * chunk
                copies.append(
                    pltpu.make_async_copy(
                        other.at[k, zl] if far else mine.at[zl],
                        out.at[pl.ds(pl.multiple_of(row, chunk), chunk)],
                        sems.at[len(copies)],
                    )
                )
    for copy in copies:
        copy.start()
    for copy in copies:
        copy.wait()


def place(chunks, other):
    pairs, chunk, columns = chunks[0].shape
    return call(
        place_kernel,
        jax.ShapeDtypeStruct((16 * chunk, columns), BF16),
        [pltpu.VMEM] * 5,
        pltpu.HBM,
        [pltpu.SemaphoreType.DMA((16,))],
        "place",
    )(*chunks, other)


def body(activations, out_grad, qkv_weight):
    core, zl = lax.axis_index("core"), lax.axis_index("zl")
    features = qkv_weight.shape[0]
    quarter = features // 4
    quarters = activations.reshape(UNIT, 2, 2, quarter).transpose(2, 1, 0, 3)
    mine = lax.all_to_all(
        quarters.reshape(4, UNIT, quarter), ("core", "zl"), 0, 0, tiled=True
    ).reshape(2 * PAIR, quarter)
    beside = swap(out_grad, "zl")
    spread = spread_out(mine, beside)
    acts = lax.all_to_all(spread, "y", 0, 0, tiled=True).reshape(8, 2, PAIR, quarter)
    near = jnp.concatenate([out_grad, beside], axis=1)
    near = order([near] + [around(near, "zh", -k) for k in (1, 2, 3)])
    received = block(qkv_weight, (1 - zl) * 2 + core, quarter)
    received = swap(after(received, near), "zl")
    acts = jnp.concatenate(
        [
            lax.dynamic_index_in_dim(acts, core ^ c, 1, keepdims=False).reshape(8 * PAIR, quarter)
            for c in range(2)
        ],
        axis=0,
    )
    far = swap(near, "core")
    own, *sends = outer(acts, near, far)
    got = [around(send, "x", k + 1) for k, send in enumerate(sends)]
    parts = multiply(near, far, qkv_weight, received, far)
    parts = parts.reshape(2, 8, PAIR, quarter).transpose(1, 0, 2, 3)
    parts = lax.all_to_all(parts.reshape(8, 2 * PAIR, quarter), "y", 0, 0, tiled=True)
    own, other = combine(own, got)
    other = swap(other, "zl")
    pair = jnp.stack([jnp.where(zl == 0, own, other), jnp.where(zl == 0, other, own)])
    chunks = [pair] + [around(pair, "x", k) for k in (1, 2, 3)]
    total = add_up(parts, chunks[3])
    parts = total.reshape(2, 2, UNIT, quarter)
    parts = jnp.concatenate([block(parts, core ^ c, 1) for c in range(2)], axis=0)
    parts = lax.all_to_all(
        parts.reshape(4, UNIT, quarter), ("core", "zl"), 0, 0, tiled=True
    ).reshape(2, 2, UNIT, quarter)
    input_grad = parts.transpose(2, 1, 0, 3).reshape(UNIT, features)
    weight_grad = place(chunks, swap(stack(chunks, parts), "core"))
    return input_grad, weight_grad


def solution(mesh):
    fine = Mesh(mesh.devices.reshape(4, 2, 4, 2, 8), ("x", "core", "zh", "zl", "y"))
    tokens, features = P(("x", "core", "zl", "y"), "zh"), P("zh", ("zl", "y"))
    return jax.shard_map(
        body,
        mesh=fine,
        in_specs=(tokens, P(("x", "core", "zh"), ("zl", "y")), features),
        out_specs=(tokens, features),
        check_vma=False,
    )
```

time: 184 us -> 123 us (0.67)
  starting transfers between devices: 6.27 us -> 76.5 us
  waiting for transfers between devices: 87.6 us -> 27.2 us
  blocking collectives: 56.9 us -> 0 us
  between operations: 14.7 us -> 0.95 us
  Pallas kernels: 0 us -> 11.1 us
  matrix products: 7.09 us -> 0 us
  other arithmetic: 3.52 us -> 0.82 us
    all_gather x1 -> x0, waiting for transfers between devices: 52.8 us -> none  [body(): lax.all_gather(activations, 'col', axis=0, tiled=True)]
    ppermute x0 -> x14, starting transfers between devices: none -> 51.5 us  [the longest x9 36.8 us: around(): lax.ppermute(value, axis, [(i, (i + step) % size) for i in range(size)])]
    unnamed x1 -> x0, blocking collectives: 38.3 us -> none
    psum x1 -> x0, waiting for transfers between devices: 32.9 us -> none  [body(): lax.psum(group_grad.astype(jnp.bfloat16), 'dp').astype(jnp.float32) / groups]
    all_to_all x0 -> x4, starting transfers between devices: none -> 25 us  [the longest x1 10.3 us: body(): lax.all_to_all(quarters.reshape(4, UNIT, quarter), ('core', 'zl'), 0, 0,...]
    all_gather x1 -> x0, blocking collectives: 18.6 us -> none  [body(): grads_all = lax.all_gather(out_grad, 'row', axis=0, tiled=True)]
    ppermute x0 -> x14, waiting for transfers between devices: none -> 14.2 us  [the longest x9 7.64 us: around(): lax.ppermute(value, axis, [(i, (i + step) % size) for i in range(size)])]
    all_to_all x0 -> x4, waiting for transfers between devices: none -> 13 us  [the longest x1 8.84 us: body(): lax.all_to_all(parts.reshape(8, 2 * PAIR, quarter), 'y', 0, 0, tiled=True)]
  transfers between devices with their start and end apart: 5 -> 18, of which waited for: 3 -> 9; matrix products, arithmetic and copies ran while one was open for 24% -> 4% of each run, Pallas kernels for 0% -> 6%
where the time goes in v3:
time: 123 us; the launch traced here: 122 us
  starting transfers between devices  76.5 us (62%)
  waiting for transfers between devices  27.2 us (22%)
  Pallas kernels  11.1 us (9%)
  local copies, waits for them, and re-layouts  5.75 us (5%)
    ppermute x9, starting transfers between devices, around(): lax.ppermute(value, axis, [(i, (i + step) % size) for i in range(size)])  36.8 us
    ppermute x5, starting transfers between devices, swap(): return lax.ppermute(value, axis, [(0, 1), (1, 0)])  14.7 us
    all_to_all x1, starting transfers between devices, body(): lax.all_to_all(quarters.reshape(4, UNIT, quarter), ('core', 'zl'), 0, 0,...  10.3 us
    all_to_all x1, waiting for transfers between devices, body(): lax.all_to_all(parts.reshape(8, 2 * PAIR, quarter), 'y', 0, 0, tiled=True)  8.84 us
    ppermute x9, waiting for transfers between devices, around(): lax.ppermute(value, axis, [(i, (i + step) % size) for i in range(size)])  7.64 us
    all_to_all x1, starting transfers between devices, body(): lax.all_to_all(parts.reshape(8, 2 * PAIR, quarter), 'y', 0, 0, tiled=True)  6.69 us
    ppermute x5, waiting for transfers between devices, swap(): return lax.ppermute(value, axis, [(0, 1), (1, 0)])  6.61 us
    all_to_all x1, starting transfers between devices, body(): lax.all_to_all(spread, 'y', 0, 0, tiled=True).reshape(8, 2, PAIR, quarter)  4.24 us
  transfers between devices with their start and end apart: 18, of which 9 were waited for; matrix products, arithmetic and copies ran while one was open for 4% of the time, Pallas kernels for 6%

profile of v3, /device:TPU:1, one launch (start us, length us, event | category | flops | bytes accessed | tf_op | source)
XLA Modules:
  0.0 122.4 jit_solution(10493361504664943251)
XLA Ops:
  2.3 10.3 %all-to-all-start.1 = ((bf16[4,20,768]{2,1,0:T(8,128)(2,1)}), bf16[4,20,768]{2,1,0:T(8,128)(2,1)S(1)}, u32[]{:S(2)}, u32[]{:S(2)}) async-start(bf16[4,20,768]{2,1,0:T(8,128)(2,1)} %bitcast.4), calls=%async_computation.1 | async-start | bytes 294912 | tf_op jit(solution)/shard_map/all_to_all | solution.py:249
  12.6 3.3 %collective-permute-start = (bf16[80,384]{1,0:T(8,128)(2,1)}, bf16[80,384]{1,0:T(8,128)(2,1)S(1)}, u32[]{:S(2)}, u32[]{:S(2)}) collective-permute-start(bf16[80,384]{1,0:T(8,128)(2,1)} %param.4), channel_id=1, source_target_pairs={{0,8},{8,0},{1,9},{9,1},{2,10},{10,2},{3,11},{11,3},{4,12},{12,4},... | collective-permute-start | bytes 184328 | tf_op jit(solution)/shard_map/ppermute | solution.py:16
  16.4 1.9 %collective-permute-done.gate = bf16[80,384]{1,0:T(8,128)(2,1)S(1)} collective-permute-done((bf16[80,384]{1,0:T(8,128)(2,1)}, bf16[80,384]{1,0:T(8,128)(2,1)S(1)}, u32[]{:S(2)}, u32[]{:S(2)}) %collective-permute-start) | collective-permute-done | bytes 61472 | tf_op jit(solution)/shard_map/ppermute | solution.py:16
  18.3 1.0 spread.1
  19.3 4.2 %all-to-all-start.2 = ((bf16[8,80,768]{2,1,0:T(8,128)(2,1)}), bf16[8,80,768]{2,1,0:T(8,128)(2,1)}, u32[]{:S(2)}, u32[]{:S(2)}) async-start(bf16[8,80,768]{2,1,0:T(8,128)(2,1)} %spread.1), calls=%async_computation.2 | async-start | bytes 1966080 | tf_op jit(solution)/shard_map/all_to_all | solution.py:254
  23.6 3.3 %collective-permute-start.3 = (bf16[80,768]{1,0:T(8,128)(2,1)S(1)}, bf16[80,768]{1,0:T(8,128)(2,1)S(1)}, u32[]{:S(2)}, u32[]{:S(2)}) collective-permute-start(bf16[80,768]{1,0:T(8,128)(2,1)S(1)} %constant_dynamic-update-slice_fusion.piece0), channel_id=1, source_target_pairs={{0,16},{16,32},{32,48},{48,0},{1,17},{17,33},{33,49},{49,1},{2,18}... | collective-permute-start | bytes 368648 | tf_op jit(solution)/shard_map/ppermute | solution.py:21
  26.9 8.5 %collective-permute-start.2 = (bf16[80,768]{1,0:T(8,128)(2,1)S(1)}, bf16[80,768]{1,0:T(8,128)(2,1)S(1)}, u32[]{:S(2)}, u32[]{:S(2)}) collective-permute-start(bf16[80,768]{1,0:T(8,128)(2,1)S(1)} %constant_dynamic-update-slice_fusion.piece0), channel_id=1, source_target_pairs={{0,32},{16,48},{32,0},{48,16},{1,33},{17,49},{33,1},{49,17},{2,34}... | collective-permute-start | bytes 368648 | tf_op jit(solution)/shard_map/ppermute | solution.py:21
  35.5 3.4 %collective-permute-start.1 = (bf16[80,768]{1,0:T(8,128)(2,1)S(1)}, bf16[80,768]{1,0:T(8,128)(2,1)S(1)}, u32[]{:S(2)}, u32[]{:S(2)}) collective-permute-start(bf16[80,768]{1,0:T(8,128)(2,1)S(1)} %constant_dynamic-update-slice_fusion.piece0), channel_id=1, source_target_pairs={{0,48},{16,0},{32,16},{48,32},{1,49},{17,1},{33,17},{49,33},{2,50}... | collective-permute-start | bytes 368648 | tf_op jit(solution)/shard_map/ppermute | solution.py:21
  39.8 1.1 collective-permute-done.2.piece2
  40.8 6.5 %collective-permute-done.1.piece1 = bf16[80,768]{1,0:T(8,128)(2,1)S(1)} collective-permute-done((bf16[80,768]{1,0:T(8,128)(2,1)S(1)}, bf16[80,768]{1,0:T(8,128)(2,1)S(1)}, u32[]{:S(2)}, u32[]{:S(2)}) %collective-permute-start.1) | collective-permute-done | bytes 122912 | tf_op jit(solution)/shard_map/ppermute | solution.py:21
  47.8 1.9 %collective-permute-start.5 = (bf16[768,384]{1,0:T(8,128)(2,1)}, bf16[768,384]{1,0:T(8,128)(2,1)}, u32[]{:S(2)}, u32[]{:S(2)}) collective-permute-start(bf16[768,384]{1,0:T(8,128)(2,1)} %constant_dynamic-slice_fusion.4), channel_id=1, source_target_pairs={{0,8},{8,0},{1,9},{9,1},{2,10},{10,2},{3,11},{11,3},{4,12},{12,4},... | collective-permute-start | bytes 1769480 | tf_op jit(solution)/shard_map/ppermute | solution.py:16
  49.7 2.9 %collective-permute-start.4 = (bf16[320,768]{1,0:T(8,128)(2,1)S(1)}, bf16[320,768]{1,0:T(8,128)(2,1)S(1)}, u32[]{:S(2)}, u32[]{:S(2)}) collective-permute-start(bf16[320,768]{1,0:T(8,128)(2,1)S(1)} %order.1.near), channel_id=1, source_target_pairs={{0,64},{64,0},{1,65},{65,1},{2,66},{66,2},{3,67},{67,3},{4,68},{68... | collective-permute-start | bytes 1474568 | tf_op jit(solution)/shard_map/ppermute | solution.py:16
  52.6 1.3 %constant_dynamic-slice_fusion.3 = (bf16[8,1,40,768]{3,2,1,0:T(8,128)(2,1)S(1)}, bf16[8,1,40,768]{3,2,1,0:T(8,128)(2,1)S(1)}) fusion(bf16[8,2,40,768]{3,2,1,0:T(8,128)(2,1)} %bitcast.5, s32[]{:T(128)S(6)} %select_n.26, s32[]{:T(128)S(6)} %select_n.27), kind=kLoop, calls=%fused_computation.10 | loop fusion | bytes 1966088 | tf_op jit(solution)/shard_map/jit(dynamic_index_in_dim)/dynamic_slice | solution.py:261
  54.1 2.6 %outer.1 = (f32[192,768]{1,0:T(8,128)S(1)}, bf16[192,768]{1,0:T(8,128)(2,1)}, bf16[192,768]{1,0:T(8,128)(2,1)}, bf16[192,768]{1,0:T(8,128)(2,1)}) custom-call(bf16[640,768]{1,0:T(8,128)(2,1)S(1)} %pad_maximum_fusion.acts, bf16[320,768]{1,0:T(8,128)(2,1)S(1)} %order.1.near, bf16[320,768]{1,0:T(8,128)(2,1)S(1)} %collective-permute-done.4.other.gate), custom_call_target="tpu_custom_call" | custom-call | flops 1000 | bytes 1000 | tf_op jit(solution)/shard_map/outer/pallas_call | solution.py:148
  56.7 3.1 %collective-permute-start.6 = (bf16[192,768]{1,0:T(8,128)(2,1)}, bf16[192,768]{1,0:T(8,128)(2,1)}, u32[]{:S(2)}, u32[]{:S(2)}) collective-permute-start(bf16[192,768]{1,0:T(8,128)(2,1)} %get-tuple-element.11), channel_id=1, source_target_pairs={{0,128},{128,256},{256,384},{384,0},{1,129},{129,257},{257,385},{3... | collective-permute-start | bytes 884744 | tf_op jit(solution)/shard_map/ppermute | solution.py:21
  59.8 4.4 %collective-permute-start.7 = (bf16[192,768]{1,0:T(8,128)(2,1)}, bf16[192,768]{1,0:T(8,128)(2,1)}, u32[]{:S(2)}, u32[]{:S(2)}) collective-permute-start(bf16[192,768]{1,0:T(8,128)(2,1)} %get-tuple-element.12), channel_id=1, source_target_pairs={{0,256},{128,384},{256,0},{384,128},{1,257},{129,385},{257,1},{385... | collective-permute-start | bytes 884744 | tf_op jit(solution)/shard_map/ppermute | solution.py:21
  64.2 3.1 %collective-permute-start.8 = (bf16[192,768]{1,0:T(8,128)(2,1)}, bf16[192,768]{1,0:T(8,128)(2,1)}, u32[]{:S(2)}, u32[]{:S(2)}) collective-permute-start(bf16[192,768]{1,0:T(8,128)(2,1)} %get-tuple-element.13), channel_id=1, source_target_pairs={{0,384},{128,0},{256,128},{384,256},{1,385},{129,1},{257,129},{385... | collective-permute-start | bytes 884744 | tf_op jit(solution)/shard_map/ppermute | solution.py:21
  67.2 2.4 %multiply.1 = bf16[640,768]{1,0:T(8,128)(2,1)S(1)} custom-call(bf16[320,768]{1,0:T(8,128)(2,1)S(1)} %order.1.near, bf16[320,768]{1,0:T(8,128)(2,1)S(1)} %collective-permute-done.4.other.gate, bf16[3072,384]{1,0:T(8,128)(2,1)S(1)} %copy-done, bf16[768,384]{1,0:T(8,128)(2,1)} %collective-permute-done.5.received, ...), custom_call_target="tpu_custom_call" | custom-call | flops 3000000000 | bytes 1000 | tf_op jit(solution)/shard_map/multiply/pallas_call | solution.py:113
  69.7 1.0 copy.9
  70.7 6.7 %all-to-all-start = ((bf16[8,80,768]{2,1,0:T(8,128)(2,1)}), bf16[8,80,768]{2,1,0:T(8,128)(2,1)S(1)}, u32[]{:S(2)}, u32[]{:S(2)}) async-start(bf16[8,80,768]{2,1,0:T(8,128)(2,1)} %bitcast.2), calls=%async_computation | async-start | bytes 1966080 | tf_op jit(solution)/shard_map/all_to_all | solution.py:271
  77.4 1.3 %combine.1 = (bf16[192,384]{1,0:T(8,128)(2,1)S(1)}, bf16[192,384]{1,0:T(8,128)(2,1)S(1)}) custom-call(f32[192,768]{1,0:T(8,128)S(1)} %copy-done.2, bf16[192,768]{1,0:T(8,128)(2,1)} %collective-permute-done.6.got1, bf16[192,768]{1,0:T(8,128)(2,1)} %collective-permute-done.7.got2, bf16[192,768]{1,0:T(8,128)(2,1)} %collective-permute-done.8.got3), custom_call_target="tpu_custom_call" | custom-call | flops 99999997952 | bytes 1000 | tf_op jit(solution)/shard_map/combine/pallas_call | solution.py:168
  78.7 3.6 %collective-permute-start.9 = (bf16[192,384]{1,0:T(8,128)(2,1)S(1)}, bf16[192,384]{1,0:T(8,128)(2,1)S(1)}, u32[]{:S(2)}, u32[]{:S(2)}) collective-permute-start(bf16[192,384]{1,0:T(8,128)(2,1)S(1)} %get-tuple-element.15), channel_id=1, source_target_pairs={{0,8},{8,0},{1,9},{9,1},{2,10},{10,2},{3,11},{11,3},{4,12},{12,4},... | collective-permute-start | bytes 442376 | tf_op jit(solution)/shard_map/ppermute | solution.py:16
  82.4 2.8 %collective-permute-done.9 = bf16[192,384]{1,0:T(8,128)(2,1)S(1)} collective-permute-done((bf16[192,384]{1,0:T(8,128)(2,1)S(1)}, bf16[192,384]{1,0:T(8,128)(2,1)S(1)}, u32[]{:S(2)}, u32[]{:S(2)}) %collective-permute-start.9) | collective-permute-done | bytes 147488 | tf_op jit(solution)/shard_map/ppermute | solution.py:16
  85.3 5.7 %collective-permute-start.10 = (bf16[2,192,384]{2,1,0:T(8,128)(2,1)S(1)}, bf16[2,192,384]{2,1,0:T(8,128)(2,1)S(1)}, u32[]{:S(2)}, u32[]{:S(2)}) collective-permute-start(bf16[2,192,384]{2,1,0:T(8,128)(2,1)S(1)} %pad_maximum_fusion.1.piece0.near), channel_id=1, source_target_pairs={{0,384},{128,0},{256,128},{384,256},{1,385},{129,1},{257,129},{385... | collective-permute-start | bytes 884744 | tf_op jit(solution)/shard_map/ppermute | solution.py:21
  90.9 3.4 %collective-permute-start.12 = (bf16[2,192,384]{2,1,0:T(8,128)(2,1)S(1)}, bf16[2,192,384]{2,1,0:T(8,128)(2,1)S(1)}, u32[]{:S(2)}, u32[]{:S(2)}) collective-permute-start(bf16[2,192,384]{2,1,0:T(8,128)(2,1)S(1)} %pad_maximum_fusion.1.piece0.near), channel_id=1, source_target_pairs={{0,256},{128,384},{256,0},{384,128},{1,257},{129,385},{257,1},{385... | collective-permute-start | bytes 884744 | tf_op jit(solution)/shard_map/ppermute | solution.py:21
  94.4 1.9 %collective-permute-start.11 = (bf16[2,192,384]{2,1,0:T(8,128)(2,1)S(1)}, bf16[2,192,384]{2,1,0:T(8,128)(2,1)S(1)}, u32[]{:S(2)}, u32[]{:S(2)}) collective-permute-start(bf16[2,192,384]{2,1,0:T(8,128)(2,1)S(1)} %pad_maximum_fusion.1.piece0.near), channel_id=1, source_target_pairs={{0,128},{128,256},{256,384},{384,0},{1,129},{129,257},{257,385},{3... | collective-permute-start | bytes 884744 | tf_op jit(solution)/shard_map/ppermute | solution.py:21
  96.3 8.8 %all-to-all-done.source = bf16[8,80,768]{2,1,0:T(8,128)(2,1)S(1)} async-done(((bf16[8,80,768]{2,1,0:T(8,128)(2,1)}), bf16[8,80,768]{2,1,0:T(8,128)(2,1)S(1)}, u32[]{:S(2)}, u32[]{:S(2)}) %all-to-all-start) | async-done | bytes 983072 | tf_op jit(solution)/shard_map/all_to_all | solution.py:271
  106.4 3.8 %all-to-all-start.3 = ((bf16[4,20,768]{2,1,0:T(8,128)(2,1)}), bf16[4,20,768]{2,1,0:T(8,128)(2,1)S(1)}, u32[]{:S(2)}, u32[]{:S(2)}) async-start(bf16[4,20,768]{2,1,0:T(8,128)(2,1)} %bitcast.10), calls=%async_computation.3 | async-start | bytes 294912 | tf_op jit(solution)/shard_map/all_to_all | solution.py:279
  110.2 3.7 %all-to-all-done.3 = bf16[4,20,768]{2,1,0:T(8,128)(2,1)S(1)} async-done(((bf16[4,20,768]{2,1,0:T(8,128)(2,1)}), bf16[4,20,768]{2,1,0:T(8,128)(2,1)S(1)}, u32[]{:S(2)}, u32[]{:S(2)}) %all-to-all-start.3) | async-done | bytes 122912 | tf_op jit(solution)/shard_map/all_to_all | solution.py:279
  114.0 3.0 %collective-permute-start.13 = (bf16[4,2,192,384]{3,2,1,0:T(8,128)(2,1)S(1)}, bf16[4,2,192,384]{3,2,1,0:T(8,128)(2,1)}, u32[]{:S(2)}, u32[]{:S(2)}) collective-permute-start(bf16[4,2,192,384]{3,2,1,0:T(8,128)(2,1)S(1)} %stack.13), channel_id=1, source_target_pairs={{0,64},{64,0},{1,65},{65,1},{2,66},{66,2},{3,67},{67,3},{4,68},{68... | collective-permute-start | bytes 3538952 | tf_op jit(solution)/shard_map/ppermute | solution.py:16
  117.8 1.8 %collective-permute-done.13.other = bf16[4,2,192,384]{3,2,1,0:T(8,128)(2,1)} collective-permute-done((bf16[4,2,192,384]{3,2,1,0:T(8,128)(2,1)S(1)}, bf16[4,2,192,384]{3,2,1,0:T(8,128)(2,1)}, u32[]{:S(2)}, u32[]{:S(2)}) %collective-permute-start.13) | collective-permute-done | bytes 1179680 | tf_op jit(solution)/shard_map/ppermute | solution.py:16
  119.6 2.8 %place.1 = bf16[3072,384]{1,0:T(8,128)(2,1)} custom-call(bf16[2,192,384]{2,1,0:T(8,128)(2,1)S(1)} %pad_maximum_fusion.1.piece0.near, bf16[2,192,384]{2,1,0:T(8,128)(2,1)S(1)} %collective-permute-done.11.piece1.next1, bf16[2,192,384]{2,1,0:T(8,128)(2,1)S(1)} %collective-permute-done.12.piece2.next2, ...), custom_call_target="tpu_custom_call" | custom-call | flops 1000 | bytes 1000 | tf_op jit(solution)/shard_map/place/pallas_call | solution.py:234
  (36 shorter events, 5.8 us)
Async XLA Ops:
  1.6 22.0 %copy-start.3 = (bf16[80,384]{1,0:T(8,128)(2,1)S(1)}, bf16[80,384]{1,0:T(8,128)(2,1)}, u32[]{:S(2)}) copy-start(bf16[80,384]{1,0:T(8,128)(2,1)} %param.4) | copy-start | bytes 184324
  2.3 36.6 %copy-start = (bf16[3072,384]{1,0:T(8,128)(2,1)S(1)}, bf16[3072,384]{1,0:T(8,128)(2,1)}, u32[]{:S(2)}) copy-start(bf16[3072,384]{1,0:T(8,128)(2,1)} %weight.1) | copy-start | bytes 7077892
  2.3 14.0 %all-to-all-start.1 = ((bf16[4,20,768]{2,1,0:T(8,128)(2,1)}), bf16[4,20,768]{2,1,0:T(8,128)(2,1)S(1)}, u32[]{:S(2)}, u32[]{:S(2)}) async-start(bf16[4,20,768]{2,1,0:T(8,128)(2,1)} %bitcast.4), calls=%async_computation.1 | async-start | bytes 294912 | tf_op jit(solution)/shard_map/all_to_all | solution.py:249
  12.6 5.7 %collective-permute-start = (bf16[80,384]{1,0:T(8,128)(2,1)}, bf16[80,384]{1,0:T(8,128)(2,1)S(1)}, u32[]{:S(2)}, u32[]{:S(2)}) collective-permute-start(bf16[80,384]{1,0:T(8,128)(2,1)} %param.4), channel_id=1, source_target_pairs={{0,8},{8,0},{1,9},{9,1},{2,10},{10,2},{3,11},{11,3},{4,12},{12,4},... | collective-permute-start | bytes 184328 | tf_op jit(solution)/shard_map/ppermute | solution.py:16
  19.3 33.3 %all-to-all-start.2 = ((bf16[8,80,768]{2,1,0:T(8,128)(2,1)}), bf16[8,80,768]{2,1,0:T(8,128)(2,1)}, u32[]{:S(2)}, u32[]{:S(2)}) async-start(bf16[8,80,768]{2,1,0:T(8,128)(2,1)} %spread.1), calls=%async_computation.2 | async-start | bytes 1966080 | tf_op jit(solution)/shard_map/all_to_all | solution.py:254
  23.6 16.1 %collective-permute-start.3 = (bf16[80,768]{1,0:T(8,128)(2,1)S(1)}, bf16[80,768]{1,0:T(8,128)(2,1)S(1)}, u32[]{:S(2)}, u32[]{:S(2)}) collective-permute-start(bf16[80,768]{1,0:T(8,128)(2,1)S(1)} %constant_dynamic-update-slice_fusion.piece0), channel_id=1, source_target_pairs={{0,16},{16,32},{32,48},{48,0},{1,17},{17,33},{33,49},{49,1},{2,18}... | collective-permute-start | bytes 368648 | tf_op jit(solution)/shard_map/ppermute | solution.py:21
  26.9 13.9 %collective-permute-start.2 = (bf16[80,768]{1,0:T(8,128)(2,1)S(1)}, bf16[80,768]{1,0:T(8,128)(2,1)S(1)}, u32[]{:S(2)}, u32[]{:S(2)}) collective-permute-start(bf16[80,768]{1,0:T(8,128)(2,1)S(1)} %constant_dynamic-update-slice_fusion.piece0), channel_id=1, source_target_pairs={{0,32},{16,48},{32,0},{48,16},{1,33},{17,49},{33,1},{49,17},{2,34}... | collective-permute-start | bytes 368648 | tf_op jit(solution)/shard_map/ppermute | solution.py:21
  35.5 11.9 %collective-permute-start.1 = (bf16[80,768]{1,0:T(8,128)(2,1)S(1)}, bf16[80,768]{1,0:T(8,128)(2,1)S(1)}, u32[]{:S(2)}, u32[]{:S(2)}) collective-permute-start(bf16[80,768]{1,0:T(8,128)(2,1)S(1)} %constant_dynamic-update-slice_fusion.piece0), channel_id=1, source_target_pairs={{0,48},{16,0},{32,16},{48,32},{1,49},{17,1},{33,17},{49,33},{2,50}... | collective-permute-start | bytes 368648 | tf_op jit(solution)/shard_map/ppermute | solution.py:21
  47.8 19.4 %collective-permute-start.5 = (bf16[768,384]{1,0:T(8,128)(2,1)}, bf16[768,384]{1,0:T(8,128)(2,1)}, u32[]{:S(2)}, u32[]{:S(2)}) collective-permute-start(bf16[768,384]{1,0:T(8,128)(2,1)} %constant_dynamic-slice_fusion.4), channel_id=1, source_target_pairs={{0,8},{8,0},{1,9},{9,1},{2,10},{10,2},{3,11},{11,3},{4,12},{12,4},... | collective-permute-start | bytes 1769480 | tf_op jit(solution)/shard_map/ppermute | solution.py:16
  49.7 4.3 %collective-permute-start.4 = (bf16[320,768]{1,0:T(8,128)(2,1)S(1)}, bf16[320,768]{1,0:T(8,128)(2,1)S(1)}, u32[]{:S(2)}, u32[]{:S(2)}) collective-permute-start(bf16[320,768]{1,0:T(8,128)(2,1)S(1)} %order.1.near), channel_id=1, source_target_pairs={{0,64},{64,0},{1,65},{65,1},{2,66},{66,2},{3,67},{67,3},{4,68},{68... | collective-permute-start | bytes 1474568 | tf_op jit(solution)/shard_map/ppermute | solution.py:16
  56.7 13.0 %copy-start.1 = (f32[192,768]{1,0:T(8,128)}, f32[192,768]{1,0:T(8,128)S(1)}, u32[]{:S(2)}) copy-start(f32[192,768]{1,0:T(8,128)S(1)} %get-tuple-element.10.own) | copy-start | bytes 1769476
  56.7 20.7 %collective-permute-start.6 = (bf16[192,768]{1,0:T(8,128)(2,1)}, bf16[192,768]{1,0:T(8,128)(2,1)}, u32[]{:S(2)}, u32[]{:S(2)}) collective-permute-start(bf16[192,768]{1,0:T(8,128)(2,1)} %get-tuple-element.11), channel_id=1, source_target_pairs={{0,128},{128,256},{256,384},{384,0},{1,129},{129,257},{257,385},{3... | collective-permute-start | bytes 884744 | tf_op jit(solution)/shard_map/ppermute | solution.py:21
  59.8 17.6 %collective-permute-start.7 = (bf16[192,768]{1,0:T(8,128)(2,1)}, bf16[192,768]{1,0:T(8,128)(2,1)}, u32[]{:S(2)}, u32[]{:S(2)}) collective-permute-start(bf16[192,768]{1,0:T(8,128)(2,1)} %get-tuple-element.12), channel_id=1, source_target_pairs={{0,256},{128,384},{256,0},{384,128},{1,257},{129,385},{257,1},{385... | collective-permute-start | bytes 884744 | tf_op jit(solution)/shard_map/ppermute | solution.py:21
  64.2 13.2 %collective-permute-start.8 = (bf16[192,768]{1,0:T(8,128)(2,1)}, bf16[192,768]{1,0:T(8,128)(2,1)}, u32[]{:S(2)}, u32[]{:S(2)}) collective-permute-start(bf16[192,768]{1,0:T(8,128)(2,1)} %get-tuple-element.13), channel_id=1, source_target_pairs={{0,384},{128,0},{256,128},{384,256},{1,385},{129,1},{257,129},{385... | collective-permute-start | bytes 884744 | tf_op jit(solution)/shard_map/ppermute | solution.py:21
  69.7 7.7 %copy-start.2 = (f32[192,768]{1,0:T(8,128)S(1)}, f32[192,768]{1,0:T(8,128)}, u32[]{:S(2)}) copy-start(f32[192,768]{1,0:T(8,128)} %copy-done.1) | copy-start | bytes 1769476
  70.7 34.5 %all-to-all-start = ((bf16[8,80,768]{2,1,0:T(8,128)(2,1)}), bf16[8,80,768]{2,1,0:T(8,128)(2,1)S(1)}, u32[]{:S(2)}, u32[]{:S(2)}) async-start(bf16[8,80,768]{2,1,0:T(8,128)(2,1)} %bitcast.2), calls=%async_computation | async-start | bytes 1966080 | tf_op jit(solution)/shard_map/all_to_all | solution.py:271
  78.7 6.5 %collective-permute-start.9 = (bf16[192,384]{1,0:T(8,128)(2,1)S(1)}, bf16[192,384]{1,0:T(8,128)(2,1)S(1)}, u32[]{:S(2)}, u32[]{:S(2)}) collective-permute-start(bf16[192,384]{1,0:T(8,128)(2,1)S(1)} %get-tuple-element.15), channel_id=1, source_target_pairs={{0,8},{8,0},{1,9},{9,1},{2,10},{10,2},{3,11},{11,3},{4,12},{12,4},... | collective-permute-start | bytes 442376 | tf_op jit(solution)/shard_map/ppermute | solution.py:16
  85.3 19.9 %collective-permute-start.10 = (bf16[2,192,384]{2,1,0:T(8,128)(2,1)S(1)}, bf16[2,192,384]{2,1,0:T(8,128)(2,1)S(1)}, u32[]{:S(2)}, u32[]{:S(2)}) collective-permute-start(bf16[2,192,384]{2,1,0:T(8,128)(2,1)S(1)} %pad_maximum_fusion.1.piece0.near), channel_id=1, source_target_pairs={{0,384},{128,0},{256,128},{384,256},{1,385},{129,1},{257,129},{385... | collective-permute-start | bytes 884744 | tf_op jit(solution)/shard_map/ppermute | solution.py:21
  90.9 19.2 %collective-permute-start.12 = (bf16[2,192,384]{2,1,0:T(8,128)(2,1)S(1)}, bf16[2,192,384]{2,1,0:T(8,128)(2,1)S(1)}, u32[]{:S(2)}, u32[]{:S(2)}) collective-permute-start(bf16[2,192,384]{2,1,0:T(8,128)(2,1)S(1)} %pad_maximum_fusion.1.piece0.near), channel_id=1, source_target_pairs={{0,256},{128,384},{256,0},{384,128},{1,257},{129,385},{257,1},{385... | collective-permute-start | bytes 884744 | tf_op jit(solution)/shard_map/ppermute | solution.py:21
  94.4 15.8 %collective-permute-start.11 = (bf16[2,192,384]{2,1,0:T(8,128)(2,1)S(1)}, bf16[2,192,384]{2,1,0:T(8,128)(2,1)S(1)}, u32[]{:S(2)}, u32[]{:S(2)}) collective-permute-start(bf16[2,192,384]{2,1,0:T(8,128)(2,1)S(1)} %pad_maximum_fusion.1.piece0.near), channel_id=1, source_target_pairs={{0,128},{128,256},{256,384},{384,0},{1,129},{129,257},{257,385},{3... | collective-permute-start | bytes 884744 | tf_op jit(solution)/shard_map/ppermute | solution.py:21
  106.4 7.5 %all-to-all-start.3 = ((bf16[4,20,768]{2,1,0:T(8,128)(2,1)}), bf16[4,20,768]{2,1,0:T(8,128)(2,1)S(1)}, u32[]{:S(2)}, u32[]{:S(2)}) async-start(bf16[4,20,768]{2,1,0:T(8,128)(2,1)} %bitcast.10), calls=%async_computation.3 | async-start | bytes 294912 | tf_op jit(solution)/shard_map/all_to_all | solution.py:279
  114.0 5.6 %collective-permute-start.13 = (bf16[4,2,192,384]{3,2,1,0:T(8,128)(2,1)S(1)}, bf16[4,2,192,384]{3,2,1,0:T(8,128)(2,1)}, u32[]{:S(2)}, u32[]{:S(2)}) collective-permute-start(bf16[4,2,192,384]{3,2,1,0:T(8,128)(2,1)S(1)} %stack.13), channel_id=1, source_target_pairs={{0,64},{64,0},{1,65},{65,1},{2,66},{66,2},{3,67},{67,3},{4,68},{68... | collective-permute-start | bytes 3538952 | tf_op jit(solution)/shard_map/ppermute | solution.py:16

commit v4 on v3

--- a/solution.py
+++ b/solution.py
@@ -86,6 +86,25 @@
         [pltpu.VMEM((4 * rows, columns), BF16), pltpu.VMEM((4 * rows, 4 * rows), F32)],
         "order",
     )(*pieces)
+
+
+def cut_kernel(weight, gate, out, sem):
+    rows = out.shape[0]
+    first = ((1 - lax.axis_index("zl")) * 2 + lax.axis_index("core")) * rows
+    copy = pltpu.make_async_copy(weight.at[pl.ds(pl.multiple_of(first, rows), rows)], out, sem)
+    copy.start()
+    copy.wait()
+
+
+def cut(weight, gate):
+    return call(
+        cut_kernel,
+        jax.ShapeDtypeStruct((weight.shape[0] // 4, weight.shape[1]), BF16),
+        [pl.ANY, pl.ANY],
+        pltpu.VMEM,
+        [pltpu.SemaphoreType.DMA],
+        "cut",
+    )(weight, gate)
 
 
 def multiply_kernel(near, other, weight, received, gate, parts, held, sem):
@@ -117,7 +136,6 @@
         pltpu.VMEM,
         [pltpu.VMEM(received.shape, BF16), pltpu.SemaphoreType.DMA],
         "multiply",
-        3 * 10**9,
     )(near, other, weight, received, gate)
 
 
@@ -254,8 +272,6 @@
     acts = lax.all_to_all(spread, "y", 0, 0, tiled=True).reshape(8, 2, PAIR, quarter)
     near = jnp.concatenate([out_grad, beside], axis=1)
     near = order([near] + [around(near, "zh", -k) for k in (1, 2, 3)])
-    received = block(qkv_weight, (1 - zl) * 2 + core, quarter)
-    received = swap(after(received, near), "zl")
     acts = jnp.concatenate(
         [
             lax.dynamic_index_in_dim(acts, core ^ c, 1, keepdims=False).reshape(8 * PAIR, quarter)
@@ -266,6 +282,7 @@
     far = swap(near, "core")
     own, *sends = outer(acts, near, far)
     got = [around(send, "x", k + 1) for k, send in enumerate(sends)]
+    received = swap(cut(qkv_weight, near), "zl")
     parts = multiply(near, far, qkv_weight, received, far)
     parts = parts.reshape(2, 8, PAIR, quarter).transpose(1, 0, 2, 3)
     parts = lax.all_to_all(parts.reshape(8, 2 * PAIR, quarter), "y", 0, 0, tiled=True)
@@ -280,7 +297,7 @@
         parts.reshape(4, UNIT, quarter), ("core", "zl"), 0, 0, tiled=True
     ).reshape(2, 2, UNIT, quarter)
     input_grad = parts.transpose(2, 1, 0, 3).reshape(UNIT, features)
-    weight_grad = place(chunks, swap(stack(chunks, parts), "core"))
+    weight_grad = place(chunks, swap(stack(chunks, input_grad), "core"))
     return input_grad, weight_grad
 
 

time: 123 us -> 122 us (level)
  blocking collectives: 0 us -> 7.17 us
  starting transfers between devices: 76.5 us -> 70 us
  local copies, waits for them, and re-layouts: 5.75 us -> 4.21 us
    all_to_all x0 -> x1, blocking collectives: none -> 7.17 us  [body(): lax.all_to_all(parts.reshape(4, UNIT, quarter), ('core', 'zl'), 0, 0, til...]
    all_to_all x1 -> x0, starting transfers between devices: 3.8 us -> none  [body(): lax.all_to_all(parts.reshape(4, UNIT, quarter), ('core', 'zl'), 0, 0, til...]
    all_to_all x1 -> x0, waiting for transfers between devices: 3.72 us -> none  [body(): lax.all_to_all(parts.reshape(4, UNIT, quarter), ('core', 'zl'), 0, 0, til...]
    ppermute x5, waiting for transfers between devices: 6.61 us -> 8.57 us  [swap(): return lax.ppermute(value, axis, [(0, 1), (1, 0)])]
    ppermute x5, starting transfers between devices: 14.7 us -> 13.1 us  [swap(): return lax.ppermute(value, axis, [(0, 1), (1, 0)])]
    all_to_all x1, waiting for transfers between devices: 8.84 us -> 10.1 us  [body(): lax.all_to_all(parts.reshape(8, 2 * PAIR, quarter), 'y', 0, 0, tiled=True)]
    pallas_call x1, Pallas kernels: 2.8 us -> 1.53 us  [place(): call(place_kernel, jax.ShapeDtypeStruct((16 * chunk, columns), BF16), [pl...]
  transfers between devices with their start and end apart: 18 -> 17, of which waited for: 9 -> 8; matrix products, arithmetic and copies ran while one was open for 4% -> 2% of each run, Pallas kernels for 6% -> 7%
where the time goes in v4:
time: 122 us; the launch traced here: 121 us
  starting transfers between devices  70 us (57%)
  waiting for transfers between devices  27.7 us (23%)
  Pallas kernels  10.8 us (9%)
  blocking collectives  7.17 us (6%)
  local copies, waits for them, and re-layouts  4.21 us (3%)
    ppermute x9, starting transfers between devices, around(): lax.ppermute(value, axis, [(i, (i + step) % size) for i in range(size)])  35.8 us
    ppermute x5, starting transfers between devices, swap(): return lax.ppermute(value, axis, [(0, 1), (1, 0)])  13.1 us
    all_to_all x1, starting transfers between devices, body(): lax.all_to_all(quarters.reshape(4, UNIT, quarter), ('core', 'zl'), 0, 0,...  10.2 us
    all_to_all x1, waiting for transfers between devices, body(): lax.all_to_all(parts.reshape(8, 2 * PAIR, quarter), 'y', 0, 0, tiled=True)  10.1 us
    ppermute x5, waiting for transfers between devices, swap(): return lax.ppermute(value, axis, [(0, 1), (1, 0)])  8.57 us
    ppermute x9, waiting for transfers between devices, around(): lax.ppermute(value, axis, [(i, (i + step) % size) for i in range(size)])  8.53 us
    all_to_all x1, blocking collectives, body(): lax.all_to_all(parts.reshape(4, UNIT, quarter), ('core', 'zl'), 0, 0, til...  7.17 us
    all_to_all x1, starting transfers between devices, body(): lax.all_to_all(parts.reshape(8, 2 * PAIR, quarter), 'y', 0, 0, tiled=True)  6.69 us
  transfers between devices with their start and end apart: 17, of which 8 were waited for; matrix products, arithmetic and copies ran while one was open for 2% of the time, Pallas kernels for 7%

profile of v4, /device:TPU:1, one launch (start us, length us, event | category | flops | bytes accessed | tf_op | source)
XLA Modules:
  0.0 121.0 jit_solution(15401761118444230496)
XLA Ops:
  0.6 1.0 reshape.44
  2.3 10.2 %all-to-all-start.1 = ((bf16[4,20,768]{2,1,0:T(8,128)(2,1)}), bf16[4,20,768]{2,1,0:T(8,128)(2,1)S(1)}, u32[]{:S(2)}, u32[]{:S(2)}) async-start(bf16[4,20,768]{2,1,0:T(8,128)(2,1)} %bitcast.4), calls=%async_computation.1 | async-start | bytes 294912 | tf_op jit(solution)/shard_map/all_to_all | solution.py:267
  12.5 3.3 %collective-permute-start = (bf16[80,384]{1,0:T(8,128)(2,1)}, bf16[80,384]{1,0:T(8,128)(2,1)S(1)}, u32[]{:S(2)}, u32[]{:S(2)}) collective-permute-start(bf16[80,384]{1,0:T(8,128)(2,1)} %param.4), channel_id=1, source_target_pairs={{0,8},{8,0},{1,9},{9,1},{2,10},{10,2},{3,11},{11,3},{4,12},{12,4},... | collective-permute-start | bytes 184328 | tf_op jit(solution)/shard_map/ppermute | solution.py:16
  16.2 1.9 %collective-permute-done.gate = bf16[80,384]{1,0:T(8,128)(2,1)S(1)} collective-permute-done((bf16[80,384]{1,0:T(8,128)(2,1)}, bf16[80,384]{1,0:T(8,128)(2,1)S(1)}, u32[]{:S(2)}, u32[]{:S(2)}) %collective-permute-start) | collective-permute-done | bytes 61472 | tf_op jit(solution)/shard_map/ppermute | solution.py:16
  18.2 1.0 spread.1
  19.2 4.2 %all-to-all-start.2 = ((bf16[8,80,768]{2,1,0:T(8,128)(2,1)}), bf16[8,80,768]{2,1,0:T(8,128)(2,1)}, u32[]{:S(2)}, u32[]{:S(2)}) async-start(bf16[8,80,768]{2,1,0:T(8,128)(2,1)} %spread.1), calls=%async_computation.2 | async-start | bytes 1966080 | tf_op jit(solution)/shard_map/all_to_all | solution.py:272
  23.5 3.3 %collective-permute-start.3 = (bf16[80,768]{1,0:T(8,128)(2,1)S(1)}, bf16[80,768]{1,0:T(8,128)(2,1)S(1)}, u32[]{:S(2)}, u32[]{:S(2)}) collective-permute-start(bf16[80,768]{1,0:T(8,128)(2,1)S(1)} %constant_dynamic-update-slice_fusion.piece0), channel_id=1, source_target_pairs={{0,16},{16,32},{32,48},{48,0},{1,17},{17,33},{33,49},{49,1},{2,18}... | collective-permute-start | bytes 368648 | tf_op jit(solution)/shard_map/ppermute | solution.py:21
  26.8 8.5 %collective-permute-start.2 = (bf16[80,768]{1,0:T(8,128)(2,1)S(1)}, bf16[80,768]{1,0:T(8,128)(2,1)S(1)}, u32[]{:S(2)}, u32[]{:S(2)}) collective-permute-start(bf16[80,768]{1,0:T(8,128)(2,1)S(1)} %constant_dynamic-update-slice_fusion.piece0), channel_id=1, source_target_pairs={{0,32},{16,48},{32,0},{48,16},{1,33},{17,49},{33,1},{49,17},{2,34}... | collective-permute-start | bytes 368648 | tf_op jit(solution)/shard_map/ppermute | solution.py:21
  35.3 3.4 %collective-permute-start.1 = (bf16[80,768]{1,0:T(8,128)(2,1)S(1)}, bf16[80,768]{1,0:T(8,128)(2,1)S(1)}, u32[]{:S(2)}, u32[]{:S(2)}) collective-permute-start(bf16[80,768]{1,0:T(8,128)(2,1)S(1)} %constant_dynamic-update-slice_fusion.piece0), channel_id=1, source_target_pairs={{0,48},{16,0},{32,16},{48,32},{1,49},{17,1},{33,17},{49,33},{2,50}... | collective-permute-start | bytes 368648 | tf_op jit(solution)/shard_map/ppermute | solution.py:21
  38.7 2.0 %collective-permute-done.2.piece2 = bf16[80,768]{1,0:T(8,128)(2,1)S(1)} collective-permute-done((bf16[80,768]{1,0:T(8,128)(2,1)S(1)}, bf16[80,768]{1,0:T(8,128)(2,1)S(1)}, u32[]{:S(2)}, u32[]{:S(2)}) %collective-permute-start.2) | collective-permute-done | bytes 122912 | tf_op jit(solution)/shard_map/ppermute | solution.py:21
  40.7 6.5 %collective-permute-done.1.piece1 = bf16[80,768]{1,0:T(8,128)(2,1)S(1)} collective-permute-done((bf16[80,768]{1,0:T(8,128)(2,1)S(1)}, bf16[80,768]{1,0:T(8,128)(2,1)S(1)}, u32[]{:S(2)}, u32[]{:S(2)}) %collective-permute-start.1) | collective-permute-done | bytes 122912 | tf_op jit(solution)/shard_map/ppermute | solution.py:21
  47.7 2.9 %collective-permute-start.4 = (bf16[320,768]{1,0:T(8,128)(2,1)S(1)}, bf16[320,768]{1,0:T(8,128)(2,1)S(1)}, u32[]{:S(2)}, u32[]{:S(2)}) collective-permute-start(bf16[320,768]{1,0:T(8,128)(2,1)S(1)} %order.1.gate.near), channel_id=1, source_target_pairs={{0,64},{64,0},{1,65},{65,1},{2,66},{66,2},{3,67},{67,3},{4,68},{68... | collective-permute-start | bytes 1474568 | tf_op jit(solution)/shard_map/ppermute | solution.py:16
  51.5 1.9 %collective-permute-start.5 = (bf16[768,384]{1,0:T(8,128)(2,1)}, bf16[768,384]{1,0:T(8,128)(2,1)}, u32[]{:S(2)}, u32[]{:S(2)}) collective-permute-start(bf16[768,384]{1,0:T(8,128)(2,1)} %cut.1), channel_id=1, source_target_pairs={{0,8},{8,0},{1,9},{9,1},{2,10},{10,2},{3,11},{11,3},{4,12},{12,4},... | collective-permute-start | bytes 1769480 | tf_op jit(solution)/shard_map/ppermute | solution.py:16
  53.5 1.3 %constant_dynamic-slice_fusion.3 = (bf16[8,1,40,768]{3,2,1,0:T(8,128)(2,1)S(1)}, bf16[8,1,40,768]{3,2,1,0:T(8,128)(2,1)S(1)}) fusion(bf16[8,2,40,768]{3,2,1,0:T(8,128)(2,1)} %bitcast.5, s32[]{:T(128)S(6)} %select_n.22, s32[]{:T(128)S(6)} %select_n.23), kind=kLoop, calls=%fused_computation.11 | loop fusion | bytes 1966088 | tf_op jit(solution)/shard_map/jit(dynamic_index_in_dim)/dynamic_slice | solution.py:277
  54.8 2.6 %outer.1 = (f32[192,768]{1,0:T(8,128)S(1)}, bf16[192,768]{1,0:T(8,128)(2,1)}, bf16[192,768]{1,0:T(8,128)(2,1)}, bf16[192,768]{1,0:T(8,128)(2,1)}) custom-call(bf16[640,768]{1,0:T(8,128)(2,1)S(1)} %pad_maximum_fusion.acts, bf16[320,768]{1,0:T(8,128)(2,1)S(1)} %order.1.gate.near, bf16[320,768]{1,0:T(8,128)(2,1)S(1)} %collective-permute-done.4.other.gate), custom_call_target="tpu_custom_call" | custom-call | flops 1000 | bytes 1000 | tf_op jit(solution)/shard_map/outer/pallas_call | solution.py:166
  57.4 3.1 %collective-permute-start.6 = (bf16[192,768]{1,0:T(8,128)(2,1)}, bf16[192,768]{1,0:T(8,128)(2,1)}, u32[]{:S(2)}, u32[]{:S(2)}) collective-permute-start(bf16[192,768]{1,0:T(8,128)(2,1)} %get-tuple-element.9), channel_id=1, source_target_pairs={{0,128},{128,256},{256,384},{384,0},{1,129},{129,257},{257,385},{3... | collective-permute-start | bytes 884744 | tf_op jit(solution)/shard_map/ppermute | solution.py:21
  60.5 4.4 %collective-permute-start.7 = (bf16[192,768]{1,0:T(8,128)(2,1)}, bf16[192,768]{1,0:T(8,128)(2,1)}, u32[]{:S(2)}, u32[]{:S(2)}) collective-permute-start(bf16[192,768]{1,0:T(8,128)(2,1)} %get-tuple-element.10), channel_id=1, source_target_pairs={{0,256},{128,384},{256,0},{384,128},{1,257},{129,385},{257,1},{385... | collective-permute-start | bytes 884744 | tf_op jit(solution)/shard_map/ppermute | solution.py:21
  64.9 3.1 %collective-permute-start.8 = (bf16[192,768]{1,0:T(8,128)(2,1)}, bf16[192,768]{1,0:T(8,128)(2,1)}, u32[]{:S(2)}, u32[]{:S(2)}) collective-permute-start(bf16[192,768]{1,0:T(8,128)(2,1)} %get-tuple-element.11), channel_id=1, source_target_pairs={{0,384},{128,0},{256,128},{384,256},{1,385},{129,1},{257,129},{385... | collective-permute-start | bytes 884744 | tf_op jit(solution)/shard_map/ppermute | solution.py:21
  68.7 2.4 %multiply.1 = bf16[640,768]{1,0:T(8,128)(2,1)S(1)} custom-call(bf16[320,768]{1,0:T(8,128)(2,1)S(1)} %order.1.gate.near, bf16[320,768]{1,0:T(8,128)(2,1)S(1)} %collective-permute-done.4.other.gate, bf16[3072,384]{1,0:T(8,128)(2,1)S(1)} %copy-done, bf16[768,384]{1,0:T(8,128)(2,1)} %collective-permute-done.5.received, ...), custom_call_target="tpu_custom_call" | custom-call | flops 1000 | bytes 1000 | tf_op jit(solution)/shard_map/multiply/pallas_call | solution.py:132
  71.1 1.0 copy.15
  72.1 6.7 %all-to-all-start = ((bf16[8,80,768]{2,1,0:T(8,128)(2,1)}), bf16[8,80,768]{2,1,0:T(8,128)(2,1)S(1)}, u32[]{:S(2)}, u32[]{:S(2)}) async-start(bf16[8,80,768]{2,1,0:T(8,128)(2,1)} %bitcast.2), calls=%async_computation | async-start | bytes 1966080 | tf_op jit(solution)/shard_map/all_to_all | solution.py:288
  78.9 1.3 %combine.1 = (bf16[192,384]{1,0:T(8,128)(2,1)S(1)}, bf16[192,384]{1,0:T(8,128)(2,1)S(1)}) custom-call(f32[192,768]{1,0:T(8,128)S(1)} %copy-done.3, bf16[192,768]{1,0:T(8,128)(2,1)} %collective-permute-done.6.got1, bf16[192,768]{1,0:T(8,128)(2,1)} %collective-permute-done.7.got2, bf16[192,768]{1,0:T(8,128)(2,1)} %collective-permute-done.8.got3), custom_call_target="tpu_custom_call" | custom-call | flops 99999997952 | bytes 1000 | tf_op jit(solution)/shard_map/combine/pallas_call | solution.py:186
  80.1 2.7 %collective-permute-start.9 = (bf16[192,384]{1,0:T(8,128)(2,1)S(1)}, bf16[192,384]{1,0:T(8,128)(2,1)S(1)}, u32[]{:S(2)}, u32[]{:S(2)}) collective-permute-start(bf16[192,384]{1,0:T(8,128)(2,1)S(1)} %get-tuple-element.13), channel_id=1, source_target_pairs={{0,8},{8,0},{1,9},{9,1},{2,10},{10,2},{3,11},{11,3},{4,12},{12,4},... | collective-permute-start | bytes 442376 | tf_op jit(solution)/shard_map/ppermute | solution.py:16
  82.8 3.5 %collective-permute-done.9 = bf16[192,384]{1,0:T(8,128)(2,1)S(1)} collective-permute-done((bf16[192,384]{1,0:T(8,128)(2,1)S(1)}, bf16[192,384]{1,0:T(8,128)(2,1)S(1)}, u32[]{:S(2)}, u32[]{:S(2)}) %collective-permute-start.9) | collective-permute-done | bytes 147488 | tf_op jit(solution)/shard_map/ppermute | solution.py:16
  86.4 4.4 %collective-permute-start.10 = (bf16[2,192,384]{2,1,0:T(8,128)(2,1)S(1)}, bf16[2,192,384]{2,1,0:T(8,128)(2,1)S(1)}, u32[]{:S(2)}, u32[]{:S(2)}) collective-permute-start(bf16[2,192,384]{2,1,0:T(8,128)(2,1)S(1)} %pad_maximum_fusion.1.piece0.near), channel_id=1, source_target_pairs={{0,384},{128,0},{256,128},{384,256},{1,385},{129,1},{257,129},{385... | collective-permute-start | bytes 884744 | tf_op jit(solution)/shard_map/ppermute | solution.py:21
  90.8 3.7 %collective-permute-start.12 = (bf16[2,192,384]{2,1,0:T(8,128)(2,1)S(1)}, bf16[2,192,384]{2,1,0:T(8,128)(2,1)S(1)}, u32[]{:S(2)}, u32[]{:S(2)}) collective-permute-start(bf16[2,192,384]{2,1,0:T(8,128)(2,1)S(1)} %pad_maximum_fusion.1.piece0.near), channel_id=1, source_target_pairs={{0,256},{128,384},{256,0},{384,128},{1,257},{129,385},{257,1},{385... | collective-permute-start | bytes 884744 | tf_op jit(solution)/shard_map/ppermute | solution.py:21
  94.5 1.9 %collective-permute-start.11 = (bf16[2,192,384]{2,1,0:T(8,128)(2,1)S(1)}, bf16[2,192,384]{2,1,0:T(8,128)(2,1)S(1)}, u32[]{:S(2)}, u32[]{:S(2)}) collective-permute-start(bf16[2,192,384]{2,1,0:T(8,128)(2,1)S(1)} %pad_maximum_fusion.1.piece0.near), channel_id=1, source_target_pairs={{0,128},{128,256},{256,384},{384,0},{1,129},{129,257},{257,385},{3... | collective-permute-start | bytes 884744 | tf_op jit(solution)/shard_map/ppermute | solution.py:21
  96.5 10.1 %all-to-all-done.source = bf16[8,80,768]{2,1,0:T(8,128)(2,1)S(1)} async-done(((bf16[8,80,768]{2,1,0:T(8,128)(2,1)}), bf16[8,80,768]{2,1,0:T(8,128)(2,1)S(1)}, u32[]{:S(2)}, u32[]{:S(2)}) %all-to-all-start) | async-done | bytes 983072 | tf_op jit(solution)/shard_map/all_to_all | solution.py:288
  107.1 7.2 %all_to_all.20 = bf16[4,20,768]{2,1,0:T(8,128)(2,1)S(1)} all-to-all(bf16[4,20,768]{2,1,0:T(8,128)(2,1)S(1)} %bitcast.26), channel_id=1, replica_groups=mesh['x'=4,'core'=2,'zh'=4,'zl'=2,'y'=8] {'core','zl'}, dimensions={0} | all-to-all | bytes 245760 | tf_op jit(solution)/shard_map/all_to_all | solution.py:296
  114.6 2.4 %collective-permute-start.13 = (bf16[4,2,192,384]{3,2,1,0:T(8,128)(2,1)S(1)}, bf16[4,2,192,384]{3,2,1,0:T(8,128)(2,1)S(1)}, u32[]{:S(2)}, u32[]{:S(2)}) collective-permute-start(bf16[4,2,192,384]{3,2,1,0:T(8,128)(2,1)S(1)} %stack.13), channel_id=1, source_target_pairs={{0,64},{64,0},{1,65},{65,1},{2,66},{66,2},{3,67},{67,3},{4,68},{68... | collective-permute-start | bytes 3538952 | tf_op jit(solution)/shard_map/ppermute | solution.py:16
  117.0 2.5 %collective-permute-done.13.other = bf16[4,2,192,384]{3,2,1,0:T(8,128)(2,1)S(1)} collective-permute-done((bf16[4,2,192,384]{3,2,1,0:T(8,128)(2,1)S(1)}, bf16[4,2,192,384]{3,2,1,0:T(8,128)(2,1)S(1)}, u32[]{:S(2)}, u32[]{:S(2)}) %collective-permute-start.13) | collective-permute-done | bytes 1179680 | tf_op jit(solution)/shard_map/ppermute | solution.py:16
  119.5 1.5 %place.1 = bf16[3072,384]{1,0:T(8,128)(2,1)} custom-call(bf16[2,192,384]{2,1,0:T(8,128)(2,1)S(1)} %pad_maximum_fusion.1.piece0.near, bf16[2,192,384]{2,1,0:T(8,128)(2,1)S(1)} %collective-permute-done.11.piece1.next1, bf16[2,192,384]{2,1,0:T(8,128)(2,1)S(1)} %collective-permute-done.12.piece2.next2, ...), custom_call_target="tpu_custom_call" | custom-call | flops 1000 | bytes 1000 | tf_op jit(solution)/shard_map/place/pallas_call | solution.py:252
  (37 shorter events, 4.2 us)
Async XLA Ops:
  1.6 21.8 %copy-start.4 = (bf16[80,384]{1,0:T(8,128)(2,1)S(1)}, bf16[80,384]{1,0:T(8,128)(2,1)}, u32[]{:S(2)}) copy-start(bf16[80,384]{1,0:T(8,128)(2,1)} %param.4) | copy-start | bytes 184324
  2.3 13.9 %all-to-all-start.1 = ((bf16[4,20,768]{2,1,0:T(8,128)(2,1)}), bf16[4,20,768]{2,1,0:T(8,128)(2,1)S(1)}, u32[]{:S(2)}, u32[]{:S(2)}) async-start(bf16[4,20,768]{2,1,0:T(8,128)(2,1)} %bitcast.4), calls=%async_computation.1 | async-start | bytes 294912 | tf_op jit(solution)/shard_map/all_to_all | solution.py:267
  12.5 5.7 %collective-permute-start = (bf16[80,384]{1,0:T(8,128)(2,1)}, bf16[80,384]{1,0:T(8,128)(2,1)S(1)}, u32[]{:S(2)}, u32[]{:S(2)}) collective-permute-start(bf16[80,384]{1,0:T(8,128)(2,1)} %param.4), channel_id=1, source_target_pairs={{0,8},{8,0},{1,9},{9,1},{2,10},{10,2},{3,11},{11,3},{4,12},{12,4},... | collective-permute-start | bytes 184328 | tf_op jit(solution)/shard_map/ppermute | solution.py:16
  16.2 34.3 %copy-start = (bf16[3072,384]{1,0:T(8,128)(2,1)S(1)}, bf16[3072,384]{1,0:T(8,128)(2,1)}, u32[]{:S(2)}) copy-start(bf16[3072,384]{1,0:T(8,128)(2,1)} %weight.3) | copy-start | bytes 7077892
  19.2 34.3 %all-to-all-start.2 = ((bf16[8,80,768]{2,1,0:T(8,128)(2,1)}), bf16[8,80,768]{2,1,0:T(8,128)(2,1)}, u32[]{:S(2)}, u32[]{:S(2)}) async-start(bf16[8,80,768]{2,1,0:T(8,128)(2,1)} %spread.1), calls=%async_computation.2 | async-start | bytes 1966080 | tf_op jit(solution)/shard_map/all_to_all | solution.py:272
  23.5 15.3 %collective-permute-start.3 = (bf16[80,768]{1,0:T(8,128)(2,1)S(1)}, bf16[80,768]{1,0:T(8,128)(2,1)S(1)}, u32[]{:S(2)}, u32[]{:S(2)}) collective-permute-start(bf16[80,768]{1,0:T(8,128)(2,1)S(1)} %constant_dynamic-update-slice_fusion.piece0), channel_id=1, source_target_pairs={{0,16},{16,32},{32,48},{48,0},{1,17},{17,33},{33,49},{49,1},{2,18}... | collective-permute-start | bytes 368648 | tf_op jit(solution)/shard_map/ppermute | solution.py:21
  26.8 13.9 %collective-permute-start.2 = (bf16[80,768]{1,0:T(8,128)(2,1)S(1)}, bf16[80,768]{1,0:T(8,128)(2,1)S(1)}, u32[]{:S(2)}, u32[]{:S(2)}) collective-permute-start(bf16[80,768]{1,0:T(8,128)(2,1)S(1)} %constant_dynamic-update-slice_fusion.piece0), channel_id=1, source_target_pairs={{0,32},{16,48},{32,0},{48,16},{1,33},{17,49},{33,1},{49,17},{2,34}... | collective-permute-start | bytes 368648 | tf_op jit(solution)/shard_map/ppermute | solution.py:21
  35.3 11.9 %collective-permute-start.1 = (bf16[80,768]{1,0:T(8,128)(2,1)S(1)}, bf16[80,768]{1,0:T(8,128)(2,1)S(1)}, u32[]{:S(2)}, u32[]{:S(2)}) collective-permute-start(bf16[80,768]{1,0:T(8,128)(2,1)S(1)} %constant_dynamic-update-slice_fusion.piece0), channel_id=1, source_target_pairs={{0,48},{16,0},{32,16},{48,32},{1,49},{17,1},{33,17},{49,33},{2,50}... | collective-permute-start | bytes 368648 | tf_op jit(solution)/shard_map/ppermute | solution.py:21
  47.7 7.1 %collective-permute-start.4 = (bf16[320,768]{1,0:T(8,128)(2,1)S(1)}, bf16[320,768]{1,0:T(8,128)(2,1)S(1)}, u32[]{:S(2)}, u32[]{:S(2)}) collective-permute-start(bf16[320,768]{1,0:T(8,128)(2,1)S(1)} %order.1.gate.near), channel_id=1, source_target_pairs={{0,64},{64,0},{1,65},{65,1},{2,66},{66,2},{3,67},{67,3},{4,68},{68... | collective-permute-start | bytes 1474568 | tf_op jit(solution)/shard_map/ppermute | solution.py:16
  51.5 17.2 %collective-permute-start.5 = (bf16[768,384]{1,0:T(8,128)(2,1)}, bf16[768,384]{1,0:T(8,128)(2,1)}, u32[]{:S(2)}, u32[]{:S(2)}) collective-permute-start(bf16[768,384]{1,0:T(8,128)(2,1)} %cut.1), channel_id=1, source_target_pairs={{0,8},{8,0},{1,9},{9,1},{2,10},{10,2},{3,11},{11,3},{4,12},{12,4},... | collective-permute-start | bytes 1769480 | tf_op jit(solution)/shard_map/ppermute | solution.py:16
  57.4 13.7 %copy-start.2 = (f32[192,768]{1,0:T(8,128)}, f32[192,768]{1,0:T(8,128)S(1)}, u32[]{:S(2)}) copy-start(f32[192,768]{1,0:T(8,128)S(1)} %get-tuple-element.8.own) | copy-start | bytes 1769476
  57.4 21.4 %collective-permute-start.6 = (bf16[192,768]{1,0:T(8,128)(2,1)}, bf16[192,768]{1,0:T(8,128)(2,1)}, u32[]{:S(2)}, u32[]{:S(2)}) collective-permute-start(bf16[192,768]{1,0:T(8,128)(2,1)} %get-tuple-element.9), channel_id=1, source_target_pairs={{0,128},{128,256},{256,384},{384,0},{1,129},{129,257},{257,385},{3... | collective-permute-start | bytes 884744 | tf_op jit(solution)/shard_map/ppermute | solution.py:21
  60.5 18.3 %collective-permute-start.7 = (bf16[192,768]{1,0:T(8,128)(2,1)}, bf16[192,768]{1,0:T(8,128)(2,1)}, u32[]{:S(2)}, u32[]{:S(2)}) collective-permute-start(bf16[192,768]{1,0:T(8,128)(2,1)} %get-tuple-element.10), channel_id=1, source_target_pairs={{0,256},{128,384},{256,0},{384,128},{1,257},{129,385},{257,1},{385... | collective-permute-start | bytes 884744 | tf_op jit(solution)/shard_map/ppermute | solution.py:21
  64.9 13.9 %collective-permute-start.8 = (bf16[192,768]{1,0:T(8,128)(2,1)}, bf16[192,768]{1,0:T(8,128)(2,1)}, u32[]{:S(2)}, u32[]{:S(2)}) collective-permute-start(bf16[192,768]{1,0:T(8,128)(2,1)} %get-tuple-element.11), channel_id=1, source_target_pairs={{0,384},{128,0},{256,128},{384,256},{1,385},{129,1},{257,129},{385... | collective-permute-start | bytes 884744 | tf_op jit(solution)/shard_map/ppermute | solution.py:21
  71.1 7.7 %copy-start.3 = (f32[192,768]{1,0:T(8,128)S(1)}, f32[192,768]{1,0:T(8,128)}, u32[]{:S(2)}) copy-start(f32[192,768]{1,0:T(8,128)} %copy-done.2) | copy-start | bytes 1769476
  72.1 34.5 %all-to-all-start = ((bf16[8,80,768]{2,1,0:T(8,128)(2,1)}), bf16[8,80,768]{2,1,0:T(8,128)(2,1)S(1)}, u32[]{:S(2)}, u32[]{:S(2)}) async-start(bf16[8,80,768]{2,1,0:T(8,128)(2,1)} %bitcast.2), calls=%async_computation | async-start | bytes 1966080 | tf_op jit(solution)/shard_map/all_to_all | solution.py:288
  80.1 6.2 %collective-permute-start.9 = (bf16[192,384]{1,0:T(8,128)(2,1)S(1)}, bf16[192,384]{1,0:T(8,128)(2,1)S(1)}, u32[]{:S(2)}, u32[]{:S(2)}) collective-permute-start(bf16[192,384]{1,0:T(8,128)(2,1)S(1)} %get-tuple-element.13), channel_id=1, source_target_pairs={{0,8},{8,0},{1,9},{9,1},{2,10},{10,2},{3,11},{11,3},{4,12},{12,4},... | collective-permute-start | bytes 442376 | tf_op jit(solution)/shard_map/ppermute | solution.py:16
  86.4 20.2 %collective-permute-start.10 = (bf16[2,192,384]{2,1,0:T(8,128)(2,1)S(1)}, bf16[2,192,384]{2,1,0:T(8,128)(2,1)S(1)}, u32[]{:S(2)}, u32[]{:S(2)}) collective-permute-start(bf16[2,192,384]{2,1,0:T(8,128)(2,1)S(1)} %pad_maximum_fusion.1.piece0.near), channel_id=1, source_target_pairs={{0,384},{128,0},{256,128},{384,256},{1,385},{129,1},{257,129},{385... | collective-permute-start | bytes 884744 | tf_op jit(solution)/shard_map/ppermute | solution.py:21
  90.8 23.7 %collective-permute-start.12 = (bf16[2,192,384]{2,1,0:T(8,128)(2,1)S(1)}, bf16[2,192,384]{2,1,0:T(8,128)(2,1)S(1)}, u32[]{:S(2)}, u32[]{:S(2)}) collective-permute-start(bf16[2,192,384]{2,1,0:T(8,128)(2,1)S(1)} %pad_maximum_fusion.1.piece0.near), channel_id=1, source_target_pairs={{0,256},{128,384},{256,0},{384,128},{1,257},{129,385},{257,1},{385... | collective-permute-start | bytes 884744 | tf_op jit(solution)/shard_map/ppermute | solution.py:21
  94.5 20.0 %collective-permute-start.11 = (bf16[2,192,384]{2,1,0:T(8,128)(2,1)S(1)}, bf16[2,192,384]{2,1,0:T(8,128)(2,1)S(1)}, u32[]{:S(2)}, u32[]{:S(2)}) collective-permute-start(bf16[2,192,384]{2,1,0:T(8,128)(2,1)S(1)} %pad_maximum_fusion.1.piece0.near), channel_id=1, source_target_pairs={{0,128},{128,256},{256,384},{384,0},{1,129},{129,257},{257,385},{3... | collective-permute-start | bytes 884744 | tf_op jit(solution)/shard_map/ppermute | solution.py:21
  114.5 6.5 %copy-start.1 = (bf16[20,3072]{1,0:T(8,128)(2,1)}, bf16[20,3072]{1,0:T(8,128)(2,1)S(1)}, u32[]{:S(2)}) copy-start(bf16[20,3072]{1,0:T(8,128)(2,1)S(1)} %reshape.53.gate) | copy-start | bytes 368644
  114.6 4.9 %collective-permute-start.13 = (bf16[4,2,192,384]{3,2,1,0:T(8,128)(2,1)S(1)}, bf16[4,2,192,384]{3,2,1,0:T(8,128)(2,1)S(1)}, u32[]{:S(2)}, u32[]{:S(2)}) collective-permute-start(bf16[4,2,192,384]{3,2,1,0:T(8,128)(2,1)S(1)} %stack.13), channel_id=1, source_target_pairs={{0,64},{64,0},{1,65},{65,1},{2,66},{66,2},{3,67},{67,3},{4,68},{68... | collective-permute-start | bytes 3538952 | tf_op jit(solution)/shard_map/ppermute | solution.py:16

commit v5 on v4

--- a/solution.py
+++ b/solution.py
@@ -184,8 +184,17 @@
 def combine(own, got):
     half = jax.ShapeDtypeStruct((own.shape[0], own.shape[1] // 2), BF16)
     return call(
-        combine_kernel, (half, half), [pltpu.VMEM] * 4, (pltpu.VMEM, pltpu.VMEM), [], "combine", 10**11
+        combine_kernel, (half, half), [pltpu.VMEM] * 4, (pltpu.VMEM, pltpu.VMEM), [], "combine"
     )(own, *got)
+
+
+def pass_on_kernel(value, out):
+    out[...] = value[...]
+
+
+def pass_on(value):
+    shape = jax.ShapeDtypeStruct(value.shape, value.dtype)
+    return call(pass_on_kernel, shape, [pltpu.VMEM], pltpu.VMEM, [], "pass_on", 10**11)(value)
 
 
 def add_up_kernel(source, gate, total, parts, sem):
@@ -287,7 +296,7 @@
     parts = parts.reshape(2, 8, PAIR, quarter).transpose(1, 0, 2, 3)
     parts = lax.all_to_all(parts.reshape(8, 2 * PAIR, quarter), "y", 0, 0, tiled=True)
     own, other = combine(own, got)
-    other = swap(other, "zl")
+    other = swap(pass_on(other), "zl")
     pair = jnp.stack([jnp.where(zl == 0, own, other), jnp.where(zl == 0, other, own)])
     chunks = [pair] + [around(pair, "x", k) for k in (1, 2, 3)]
     total = add_up(parts, chunks[3])

time: 122 us -> 122 us (level)
  no operation moved by 1% of the time
where the time goes in v5:
time: 122 us; the launch traced here: 121 us
  starting transfers between devices  70 us (57%)
  waiting for transfers between devices  27.7 us (23%)
  Pallas kernels  10.8 us (9%)
  blocking collectives  7.17 us (6%)
  local copies, waits for them, and re-layouts  4.21 us (3%)
    ppermute x9, starting transfers between devices, around(): lax.ppermute(value, axis, [(i, (i + step) % size) for i in range(size)])  35.8 us
    ppermute x5, starting transfers between devices, swap(): return lax.ppermute(value, axis, [(0, 1), (1, 0)])  13.1 us
    all_to_all x1, starting transfers between devices, body(): lax.all_to_all(quarters.reshape(4, UNIT, quarter), ('core', 'zl'), 0, 0,...  10.2 us
    all_to_all x1, waiting for transfers between devices, body(): lax.all_to_all(parts.reshape(8, 2 * PAIR, quarter), 'y', 0, 0, tiled=True)  10.1 us
    ppermute x5, waiting for transfers between devices, swap(): return lax.ppermute(value, axis, [(0, 1), (1, 0)])  8.57 us
    ppermute x9, waiting for transfers between devices, around(): lax.ppermute(value, axis, [(i, (i + step) % size) for i in range(size)])  8.53 us
    all_to_all x1, blocking collectives, body(): lax.all_to_all(parts.reshape(4, UNIT, quarter), ('core', 'zl'), 0, 0, til...  7.17 us
    all_to_all x1, starting transfers between devices, body(): lax.all_to_all(parts.reshape(8, 2 * PAIR, quarter), 'y', 0, 0, tiled=True)  6.69 us
  transfers between devices with their start and end apart: 17, of which 8 were waited for; matrix products, arithmetic and copies ran while one was open for 2% of the time, Pallas kernels for 7%

profile of v5, /device:TPU:1, one launch (start us, length us, event | category | flops | bytes accessed | tf_op | source)
XLA Modules:
  0.0 121.0 jit_solution(1888971891204204650)
XLA Ops:
  0.6 1.0 reshape.44
  2.3 10.2 %all-to-all-start.1 = ((bf16[4,20,768]{2,1,0:T(8,128)(2,1)}), bf16[4,20,768]{2,1,0:T(8,128)(2,1)S(1)}, u32[]{:S(2)}, u32[]{:S(2)}) async-start(bf16[4,20,768]{2,1,0:T(8,128)(2,1)} %bitcast.4), calls=%async_computation.1 | async-start | bytes 294912 | tf_op jit(solution)/shard_map/all_to_all | solution.py:276
  12.5 3.3 %collective-permute-start = (bf16[80,384]{1,0:T(8,128)(2,1)}, bf16[80,384]{1,0:T(8,128)(2,1)S(1)}, u32[]{:S(2)}, u32[]{:S(2)}) collective-permute-start(bf16[80,384]{1,0:T(8,128)(2,1)} %param.4), channel_id=1, source_target_pairs={{0,8},{8,0},{1,9},{9,1},{2,10},{10,2},{3,11},{11,3},{4,12},{12,4},... | collective-permute-start | bytes 184328 | tf_op jit(solution)/shard_map/ppermute | solution.py:16
  16.2 1.9 %collective-permute-done.gate = bf16[80,384]{1,0:T(8,128)(2,1)S(1)} collective-permute-done((bf16[80,384]{1,0:T(8,128)(2,1)}, bf16[80,384]{1,0:T(8,128)(2,1)S(1)}, u32[]{:S(2)}, u32[]{:S(2)}) %collective-permute-start) | collective-permute-done | bytes 61472 | tf_op jit(solution)/shard_map/ppermute | solution.py:16
  18.2 1.0 spread.1
  19.2 4.2 %all-to-all-start.2 = ((bf16[8,80,768]{2,1,0:T(8,128)(2,1)}), bf16[8,80,768]{2,1,0:T(8,128)(2,1)}, u32[]{:S(2)}, u32[]{:S(2)}) async-start(bf16[8,80,768]{2,1,0:T(8,128)(2,1)} %spread.1), calls=%async_computation.2 | async-start | bytes 1966080 | tf_op jit(solution)/shard_map/all_to_all | solution.py:281
  23.5 3.3 %collective-permute-start.3 = (bf16[80,768]{1,0:T(8,128)(2,1)S(1)}, bf16[80,768]{1,0:T(8,128)(2,1)S(1)}, u32[]{:S(2)}, u32[]{:S(2)}) collective-permute-start(bf16[80,768]{1,0:T(8,128)(2,1)S(1)} %constant_dynamic-update-slice_fusion.piece0), channel_id=1, source_target_pairs={{0,16},{16,32},{32,48},{48,0},{1,17},{17,33},{33,49},{49,1},{2,18}... | collective-permute-start | bytes 368648 | tf_op jit(solution)/shard_map/ppermute | solution.py:21
  26.8 8.5 %collective-permute-start.2 = (bf16[80,768]{1,0:T(8,128)(2,1)S(1)}, bf16[80,768]{1,0:T(8,128)(2,1)S(1)}, u32[]{:S(2)}, u32[]{:S(2)}) collective-permute-start(bf16[80,768]{1,0:T(8,128)(2,1)S(1)} %constant_dynamic-update-slice_fusion.piece0), channel_id=1, source_target_pairs={{0,32},{16,48},{32,0},{48,16},{1,33},{17,49},{33,1},{49,17},{2,34}... | collective-permute-start | bytes 368648 | tf_op jit(solution)/shard_map/ppermute | solution.py:21
  35.3 3.4 %collective-permute-start.1 = (bf16[80,768]{1,0:T(8,128)(2,1)S(1)}, bf16[80,768]{1,0:T(8,128)(2,1)S(1)}, u32[]{:S(2)}, u32[]{:S(2)}) collective-permute-start(bf16[80,768]{1,0:T(8,128)(2,1)S(1)} %constant_dynamic-update-slice_fusion.piece0), channel_id=1, source_target_pairs={{0,48},{16,0},{32,16},{48,32},{1,49},{17,1},{33,17},{49,33},{2,50}... | collective-permute-start | bytes 368648 | tf_op jit(solution)/shard_map/ppermute | solution.py:21
  38.7 2.0 %collective-permute-done.2.piece2 = bf16[80,768]{1,0:T(8,128)(2,1)S(1)} collective-permute-done((bf16[80,768]{1,0:T(8,128)(2,1)S(1)}, bf16[80,768]{1,0:T(8,128)(2,1)S(1)}, u32[]{:S(2)}, u32[]{:S(2)}) %collective-permute-start.2) | collective-permute-done | bytes 122912 | tf_op jit(solution)/shard_map/ppermute | solution.py:21
  40.7 6.5 %collective-permute-done.1.piece1 = bf16[80,768]{1,0:T(8,128)(2,1)S(1)} collective-permute-done((bf16[80,768]{1,0:T(8,128)(2,1)S(1)}, bf16[80,768]{1,0:T(8,128)(2,1)S(1)}, u32[]{:S(2)}, u32[]{:S(2)}) %collective-permute-start.1) | collective-permute-done | bytes 122912 | tf_op jit(solution)/shard_map/ppermute | solution.py:21
  47.7 2.9 %collective-permute-start.4 = (bf16[320,768]{1,0:T(8,128)(2,1)S(1)}, bf16[320,768]{1,0:T(8,128)(2,1)S(1)}, u32[]{:S(2)}, u32[]{:S(2)}) collective-permute-start(bf16[320,768]{1,0:T(8,128)(2,1)S(1)} %order.1.gate.near), channel_id=1, source_target_pairs={{0,64},{64,0},{1,65},{65,1},{2,66},{66,2},{3,67},{67,3},{4,68},{68... | collective-permute-start | bytes 1474568 | tf_op jit(solution)/shard_map/ppermute | solution.py:16
  51.5 1.9 %collective-permute-start.5 = (bf16[768,384]{1,0:T(8,128)(2,1)}, bf16[768,384]{1,0:T(8,128)(2,1)}, u32[]{:S(2)}, u32[]{:S(2)}) collective-permute-start(bf16[768,384]{1,0:T(8,128)(2,1)} %cut.1), channel_id=1, source_target_pairs={{0,8},{8,0},{1,9},{9,1},{2,10},{10,2},{3,11},{11,3},{4,12},{12,4},... | collective-permute-start | bytes 1769480 | tf_op jit(solution)/shard_map/ppermute | solution.py:16
  53.5 1.3 %constant_dynamic-slice_fusion.3 = (bf16[8,1,40,768]{3,2,1,0:T(8,128)(2,1)S(1)}, bf16[8,1,40,768]{3,2,1,0:T(8,128)(2,1)S(1)}) fusion(bf16[8,2,40,768]{3,2,1,0:T(8,128)(2,1)} %bitcast.5, s32[]{:T(128)S(6)} %select_n.22, s32[]{:T(128)S(6)} %select_n.23), kind=kLoop, calls=%fused_computation.11 | loop fusion | bytes 1966088 | tf_op jit(solution)/shard_map/jit(dynamic_index_in_dim)/dynamic_slice | solution.py:286
  54.8 2.6 %outer.1 = (f32[192,768]{1,0:T(8,128)S(1)}, bf16[192,768]{1,0:T(8,128)(2,1)}, bf16[192,768]{1,0:T(8,128)(2,1)}, bf16[192,768]{1,0:T(8,128)(2,1)}) custom-call(bf16[640,768]{1,0:T(8,128)(2,1)S(1)} %pad_maximum_fusion.acts, bf16[320,768]{1,0:T(8,128)(2,1)S(1)} %order.1.gate.near, bf16[320,768]{1,0:T(8,128)(2,1)S(1)} %collective-permute-done.4.other.gate), custom_call_target="tpu_custom_call" | custom-call | flops 1000 | bytes 1000 | tf_op jit(solution)/shard_map/outer/pallas_call | solution.py:166
  57.4 3.1 %collective-permute-start.6 = (bf16[192,768]{1,0:T(8,128)(2,1)}, bf16[192,768]{1,0:T(8,128)(2,1)}, u32[]{:S(2)}, u32[]{:S(2)}) collective-permute-start(bf16[192,768]{1,0:T(8,128)(2,1)} %get-tuple-element.9), channel_id=1, source_target_pairs={{0,128},{128,256},{256,384},{384,0},{1,129},{129,257},{257,385},{3... | collective-permute-start | bytes 884744 | tf_op jit(solution)/shard_map/ppermute | solution.py:21
  60.5 4.4 %collective-permute-start.7 = (bf16[192,768]{1,0:T(8,128)(2,1)}, bf16[192,768]{1,0:T(8,128)(2,1)}, u32[]{:S(2)}, u32[]{:S(2)}) collective-permute-start(bf16[192,768]{1,0:T(8,128)(2,1)} %get-tuple-element.10), channel_id=1, source_target_pairs={{0,256},{128,384},{256,0},{384,128},{1,257},{129,385},{257,1},{385... | collective-permute-start | bytes 884744 | tf_op jit(solution)/shard_map/ppermute | solution.py:21
  64.9 3.1 %collective-permute-start.8 = (bf16[192,768]{1,0:T(8,128)(2,1)}, bf16[192,768]{1,0:T(8,128)(2,1)}, u32[]{:S(2)}, u32[]{:S(2)}) collective-permute-start(bf16[192,768]{1,0:T(8,128)(2,1)} %get-tuple-element.11), channel_id=1, source_target_pairs={{0,384},{128,0},{256,128},{384,256},{1,385},{129,1},{257,129},{385... | collective-permute-start | bytes 884744 | tf_op jit(solution)/shard_map/ppermute | solution.py:21
  68.7 2.4 %multiply.1 = bf16[640,768]{1,0:T(8,128)(2,1)S(1)} custom-call(bf16[320,768]{1,0:T(8,128)(2,1)S(1)} %order.1.gate.near, bf16[320,768]{1,0:T(8,128)(2,1)S(1)} %collective-permute-done.4.other.gate, bf16[3072,384]{1,0:T(8,128)(2,1)S(1)} %copy-done, bf16[768,384]{1,0:T(8,128)(2,1)} %collective-permute-done.5.received, ...), custom_call_target="tpu_custom_call" | custom-call | flops 1000 | bytes 1000 | tf_op jit(solution)/shard_map/multiply/pallas_call | solution.py:132
  71.1 1.0 copy.15
  72.1 6.7 %all-to-all-start = ((bf16[8,80,768]{2,1,0:T(8,128)(2,1)}), bf16[8,80,768]{2,1,0:T(8,128)(2,1)S(1)}, u32[]{:S(2)}, u32[]{:S(2)}) async-start(bf16[8,80,768]{2,1,0:T(8,128)(2,1)} %bitcast.2), calls=%async_computation | async-start | bytes 1966080 | tf_op jit(solution)/shard_map/all_to_all | solution.py:297
  78.9 1.3 %combine.1 = (bf16[192,384]{1,0:T(8,128)(2,1)S(1)}, bf16[192,384]{1,0:T(8,128)(2,1)S(1)}) custom-call(f32[192,768]{1,0:T(8,128)S(1)} %copy-done.3, bf16[192,768]{1,0:T(8,128)(2,1)} %collective-permute-done.6.got1, bf16[192,768]{1,0:T(8,128)(2,1)} %collective-permute-done.7.got2, bf16[192,768]{1,0:T(8,128)(2,1)} %collective-permute-done.8.got3), custom_call_target="tpu_custom_call" | custom-call | flops 1000 | bytes 1000 | tf_op jit(solution)/shard_map/combine/pallas_call | solution.py:186
  80.2 2.7 %collective-permute-start.9 = (bf16[192,384]{1,0:T(8,128)(2,1)S(1)}, bf16[192,384]{1,0:T(8,128)(2,1)S(1)}, u32[]{:S(2)}, u32[]{:S(2)}) collective-permute-start(bf16[192,384]{1,0:T(8,128)(2,1)S(1)} %pass_on.1), channel_id=1, source_target_pairs={{0,8},{8,0},{1,9},{9,1},{2,10},{10,2},{3,11},{11,3},{4,12},{12,4},... | collective-permute-start | bytes 442376 | tf_op jit(solution)/shard_map/ppermute | solution.py:16
  82.9 3.5 %collective-permute-done.9 = bf16[192,384]{1,0:T(8,128)(2,1)S(1)} collective-permute-done((bf16[192,384]{1,0:T(8,128)(2,1)S(1)}, bf16[192,384]{1,0:T(8,128)(2,1)S(1)}, u32[]{:S(2)}, u32[]{:S(2)}) %collective-permute-start.9) | collective-permute-done | bytes 147488 | tf_op jit(solution)/shard_map/ppermute | solution.py:16
  86.4 4.4 %collective-permute-start.10 = (bf16[2,192,384]{2,1,0:T(8,128)(2,1)S(1)}, bf16[2,192,384]{2,1,0:T(8,128)(2,1)S(1)}, u32[]{:S(2)}, u32[]{:S(2)}) collective-permute-start(bf16[2,192,384]{2,1,0:T(8,128)(2,1)S(1)} %pad_maximum_fusion.1.piece0.near), channel_id=1, source_target_pairs={{0,384},{128,0},{256,128},{384,256},{1,385},{129,1},{257,129},{385... | collective-permute-start | bytes 884744 | tf_op jit(solution)/shard_map/ppermute | solution.py:21
  90.8 3.7 %collective-permute-start.12 = (bf16[2,192,384]{2,1,0:T(8,128)(2,1)S(1)}, bf16[2,192,384]{2,1,0:T(8,128)(2,1)S(1)}, u32[]{:S(2)}, u32[]{:S(2)}) collective-permute-start(bf16[2,192,384]{2,1,0:T(8,128)(2,1)S(1)} %pad_maximum_fusion.1.piece0.near), channel_id=1, source_target_pairs={{0,256},{128,384},{256,0},{384,128},{1,257},{129,385},{257,1},{385... | collective-permute-start | bytes 884744 | tf_op jit(solution)/shard_map/ppermute | solution.py:21
  94.6 1.9 %collective-permute-start.11 = (bf16[2,192,384]{2,1,0:T(8,128)(2,1)S(1)}, bf16[2,192,384]{2,1,0:T(8,128)(2,1)S(1)}, u32[]{:S(2)}, u32[]{:S(2)}) collective-permute-start(bf16[2,192,384]{2,1,0:T(8,128)(2,1)S(1)} %pad_maximum_fusion.1.piece0.near), channel_id=1, source_target_pairs={{0,128},{128,256},{256,384},{384,0},{1,129},{129,257},{257,385},{3... | collective-permute-start | bytes 884744 | tf_op jit(solution)/shard_map/ppermute | solution.py:21
  96.5 10.1 %all-to-all-done.source = bf16[8,80,768]{2,1,0:T(8,128)(2,1)S(1)} async-done(((bf16[8,80,768]{2,1,0:T(8,128)(2,1)}), bf16[8,80,768]{2,1,0:T(8,128)(2,1)S(1)}, u32[]{:S(2)}, u32[]{:S(2)}) %all-to-all-start) | async-done | bytes 983072 | tf_op jit(solution)/shard_map/all_to_all | solution.py:297
  107.1 7.2 %all_to_all.20 = bf16[4,20,768]{2,1,0:T(8,128)(2,1)S(1)} all-to-all(bf16[4,20,768]{2,1,0:T(8,128)(2,1)S(1)} %bitcast.26), channel_id=1, replica_groups=mesh['x'=4,'core'=2,'zh'=4,'zl'=2,'y'=8] {'core','zl'}, dimensions={0} | all-to-all | bytes 245760 | tf_op jit(solution)/shard_map/all_to_all | solution.py:305
  114.6 2.4 %collective-permute-start.13 = (bf16[4,2,192,384]{3,2,1,0:T(8,128)(2,1)S(1)}, bf16[4,2,192,384]{3,2,1,0:T(8,128)(2,1)S(1)}, u32[]{:S(2)}, u32[]{:S(2)}) collective-permute-start(bf16[4,2,192,384]{3,2,1,0:T(8,128)(2,1)S(1)} %stack.13), channel_id=1, source_target_pairs={{0,64},{64,0},{1,65},{65,1},{2,66},{66,2},{3,67},{67,3},{4,68},{68... | collective-permute-start | bytes 3538952 | tf_op jit(solution)/shard_map/ppermute | solution.py:16
  117.0 2.5 %collective-permute-done.13.other = bf16[4,2,192,384]{3,2,1,0:T(8,128)(2,1)S(1)} collective-permute-done((bf16[4,2,192,384]{3,2,1,0:T(8,128)(2,1)S(1)}, bf16[4,2,192,384]{3,2,1,0:T(8,128)(2,1)S(1)}, u32[]{:S(2)}, u32[]{:S(2)}) %collective-permute-start.13) | collective-permute-done | bytes 1179680 | tf_op jit(solution)/shard_map/ppermute | solution.py:16
  119.5 1.5 %place.1 = bf16[3072,384]{1,0:T(8,128)(2,1)} custom-call(bf16[2,192,384]{2,1,0:T(8,128)(2,1)S(1)} %pad_maximum_fusion.1.piece0.near, bf16[2,192,384]{2,1,0:T(8,128)(2,1)S(1)} %collective-permute-done.11.piece1.next1, bf16[2,192,384]{2,1,0:T(8,128)(2,1)S(1)} %collective-permute-done.12.piece2.next2, ...), custom_call_target="tpu_custom_call" | custom-call | flops 1000 | bytes 1000 | tf_op jit(solution)/shard_map/place/pallas_call | solution.py:261
  (38 shorter events, 4.2 us)
Async XLA Ops:
  1.6 21.8 %copy-start.4 = (bf16[80,384]{1,0:T(8,128)(2,1)S(1)}, bf16[80,384]{1,0:T(8,128)(2,1)}, u32[]{:S(2)}) copy-start(bf16[80,384]{1,0:T(8,128)(2,1)} %param.4) | copy-start | bytes 184324
  2.3 13.9 %all-to-all-start.1 = ((bf16[4,20,768]{2,1,0:T(8,128)(2,1)}), bf16[4,20,768]{2,1,0:T(8,128)(2,1)S(1)}, u32[]{:S(2)}, u32[]{:S(2)}) async-start(bf16[4,20,768]{2,1,0:T(8,128)(2,1)} %bitcast.4), calls=%async_computation.1 | async-start | bytes 294912 | tf_op jit(solution)/shard_map/all_to_all | solution.py:276
  12.5 5.7 %collective-permute-start = (bf16[80,384]{1,0:T(8,128)(2,1)}, bf16[80,384]{1,0:T(8,128)(2,1)S(1)}, u32[]{:S(2)}, u32[]{:S(2)}) collective-permute-start(bf16[80,384]{1,0:T(8,128)(2,1)} %param.4), channel_id=1, source_target_pairs={{0,8},{8,0},{1,9},{9,1},{2,10},{10,2},{3,11},{11,3},{4,12},{12,4},... | collective-permute-start | bytes 184328 | tf_op jit(solution)/shard_map/ppermute | solution.py:16
  16.2 34.3 %copy-start = (bf16[3072,384]{1,0:T(8,128)(2,1)S(1)}, bf16[3072,384]{1,0:T(8,128)(2,1)}, u32[]{:S(2)}) copy-start(bf16[3072,384]{1,0:T(8,128)(2,1)} %weight.3) | copy-start | bytes 7077892
  19.2 34.3 %all-to-all-start.2 = ((bf16[8,80,768]{2,1,0:T(8,128)(2,1)}), bf16[8,80,768]{2,1,0:T(8,128)(2,1)}, u32[]{:S(2)}, u32[]{:S(2)}) async-start(bf16[8,80,768]{2,1,0:T(8,128)(2,1)} %spread.1), calls=%async_computation.2 | async-start | bytes 1966080 | tf_op jit(solution)/shard_map/all_to_all | solution.py:281
  23.5 15.3 %collective-permute-start.3 = (bf16[80,768]{1,0:T(8,128)(2,1)S(1)}, bf16[80,768]{1,0:T(8,128)(2,1)S(1)}, u32[]{:S(2)}, u32[]{:S(2)}) collective-permute-start(bf16[80,768]{1,0:T(8,128)(2,1)S(1)} %constant_dynamic-update-slice_fusion.piece0), channel_id=1, source_target_pairs={{0,16},{16,32},{32,48},{48,0},{1,17},{17,33},{33,49},{49,1},{2,18}... | collective-permute-start | bytes 368648 | tf_op jit(solution)/shard_map/ppermute | solution.py:21
  26.8 13.9 %collective-permute-start.2 = (bf16[80,768]{1,0:T(8,128)(2,1)S(1)}, bf16[80,768]{1,0:T(8,128)(2,1)S(1)}, u32[]{:S(2)}, u32[]{:S(2)}) collective-permute-start(bf16[80,768]{1,0:T(8,128)(2,1)S(1)} %constant_dynamic-update-slice_fusion.piece0), channel_id=1, source_target_pairs={{0,32},{16,48},{32,0},{48,16},{1,33},{17,49},{33,1},{49,17},{2,34}... | collective-permute-start | bytes 368648 | tf_op jit(solution)/shard_map/ppermute | solution.py:21
  35.3 11.9 %collective-permute-start.1 = (bf16[80,768]{1,0:T(8,128)(2,1)S(1)}, bf16[80,768]{1,0:T(8,128)(2,1)S(1)}, u32[]{:S(2)}, u32[]{:S(2)}) collective-permute-start(bf16[80,768]{1,0:T(8,128)(2,1)S(1)} %constant_dynamic-update-slice_fusion.piece0), channel_id=1, source_target_pairs={{0,48},{16,0},{32,16},{48,32},{1,49},{17,1},{33,17},{49,33},{2,50}... | collective-permute-start | bytes 368648 | tf_op jit(solution)/shard_map/ppermute | solution.py:21
  47.7 7.1 %collective-permute-start.4 = (bf16[320,768]{1,0:T(8,128)(2,1)S(1)}, bf16[320,768]{1,0:T(8,128)(2,1)S(1)}, u32[]{:S(2)}, u32[]{:S(2)}) collective-permute-start(bf16[320,768]{1,0:T(8,128)(2,1)S(1)} %order.1.gate.near), channel_id=1, source_target_pairs={{0,64},{64,0},{1,65},{65,1},{2,66},{66,2},{3,67},{67,3},{4,68},{68... | collective-permute-start | bytes 1474568 | tf_op jit(solution)/shard_map/ppermute | solution.py:16
  51.5 17.2 %collective-permute-start.5 = (bf16[768,384]{1,0:T(8,128)(2,1)}, bf16[768,384]{1,0:T(8,128)(2,1)}, u32[]{:S(2)}, u32[]{:S(2)}) collective-permute-start(bf16[768,384]{1,0:T(8,128)(2,1)} %cut.1), channel_id=1, source_target_pairs={{0,8},{8,0},{1,9},{9,1},{2,10},{10,2},{3,11},{11,3},{4,12},{12,4},... | collective-permute-start | bytes 1769480 | tf_op jit(solution)/shard_map/ppermute | solution.py:16
  57.4 13.7 %copy-start.2 = (f32[192,768]{1,0:T(8,128)}, f32[192,768]{1,0:T(8,128)S(1)}, u32[]{:S(2)}) copy-start(f32[192,768]{1,0:T(8,128)S(1)} %get-tuple-element.8.own) | copy-start | bytes 1769476
  57.4 21.4 %collective-permute-start.6 = (bf16[192,768]{1,0:T(8,128)(2,1)}, bf16[192,768]{1,0:T(8,128)(2,1)}, u32[]{:S(2)}, u32[]{:S(2)}) collective-permute-start(bf16[192,768]{1,0:T(8,128)(2,1)} %get-tuple-element.9), channel_id=1, source_target_pairs={{0,128},{128,256},{256,384},{384,0},{1,129},{129,257},{257,385},{3... | collective-permute-start | bytes 884744 | tf_op jit(solution)/shard_map/ppermute | solution.py:21
  60.5 18.3 %collective-permute-start.7 = (bf16[192,768]{1,0:T(8,128)(2,1)}, bf16[192,768]{1,0:T(8,128)(2,1)}, u32[]{:S(2)}, u32[]{:S(2)}) collective-permute-start(bf16[192,768]{1,0:T(8,128)(2,1)} %get-tuple-element.10), channel_id=1, source_target_pairs={{0,256},{128,384},{256,0},{384,128},{1,257},{129,385},{257,1},{385... | collective-permute-start | bytes 884744 | tf_op jit(solution)/shard_map/ppermute | solution.py:21
  64.9 13.9 %collective-permute-start.8 = (bf16[192,768]{1,0:T(8,128)(2,1)}, bf16[192,768]{1,0:T(8,128)(2,1)}, u32[]{:S(2)}, u32[]{:S(2)}) collective-permute-start(bf16[192,768]{1,0:T(8,128)(2,1)} %get-tuple-element.11), channel_id=1, source_target_pairs={{0,384},{128,0},{256,128},{384,256},{1,385},{129,1},{257,129},{385... | collective-permute-start | bytes 884744 | tf_op jit(solution)/shard_map/ppermute | solution.py:21
  71.1 7.7 %copy-start.3 = (f32[192,768]{1,0:T(8,128)S(1)}, f32[192,768]{1,0:T(8,128)}, u32[]{:S(2)}) copy-start(f32[192,768]{1,0:T(8,128)} %copy-done.2) | copy-start | bytes 1769476
  72.1 34.5 %all-to-all-start = ((bf16[8,80,768]{2,1,0:T(8,128)(2,1)}), bf16[8,80,768]{2,1,0:T(8,128)(2,1)S(1)}, u32[]{:S(2)}, u32[]{:S(2)}) async-start(bf16[8,80,768]{2,1,0:T(8,128)(2,1)} %bitcast.2), calls=%async_computation | async-start | bytes 1966080 | tf_op jit(solution)/shard_map/all_to_all | solution.py:297
  80.2 6.2 %collective-permute-start.9 = (bf16[192,384]{1,0:T(8,128)(2,1)S(1)}, bf16[192,384]{1,0:T(8,128)(2,1)S(1)}, u32[]{:S(2)}, u32[]{:S(2)}) collective-permute-start(bf16[192,384]{1,0:T(8,128)(2,1)S(1)} %pass_on.1), channel_id=1, source_target_pairs={{0,8},{8,0},{1,9},{9,1},{2,10},{10,2},{3,11},{11,3},{4,12},{12,4},... | collective-permute-start | bytes 442376 | tf_op jit(solution)/shard_map/ppermute | solution.py:16
  86.4 20.2 %collective-permute-start.10 = (bf16[2,192,384]{2,1,0:T(8,128)(2,1)S(1)}, bf16[2,192,384]{2,1,0:T(8,128)(2,1)S(1)}, u32[]{:S(2)}, u32[]{:S(2)}) collective-permute-start(bf16[2,192,384]{2,1,0:T(8,128)(2,1)S(1)} %pad_maximum_fusion.1.piece0.near), channel_id=1, source_target_pairs={{0,384},{128,0},{256,128},{384,256},{1,385},{129,1},{257,129},{385... | collective-permute-start | bytes 884744 | tf_op jit(solution)/shard_map/ppermute | solution.py:21
  90.8 23.7 %collective-permute-start.12 = (bf16[2,192,384]{2,1,0:T(8,128)(2,1)S(1)}, bf16[2,192,384]{2,1,0:T(8,128)(2,1)S(1)}, u32[]{:S(2)}, u32[]{:S(2)}) collective-permute-start(bf16[2,192,384]{2,1,0:T(8,128)(2,1)S(1)} %pad_maximum_fusion.1.piece0.near), channel_id=1, source_target_pairs={{0,256},{128,384},{256,0},{384,128},{1,257},{129,385},{257,1},{385... | collective-permute-start | bytes 884744 | tf_op jit(solution)/shard_map/ppermute | solution.py:21
  94.6 20.0 %collective-permute-start.11 = (bf16[2,192,384]{2,1,0:T(8,128)(2,1)S(1)}, bf16[2,192,384]{2,1,0:T(8,128)(2,1)S(1)}, u32[]{:S(2)}, u32[]{:S(2)}) collective-permute-start(bf16[2,192,384]{2,1,0:T(8,128)(2,1)S(1)} %pad_maximum_fusion.1.piece0.near), channel_id=1, source_target_pairs={{0,128},{128,256},{256,384},{384,0},{1,129},{129,257},{257,385},{3... | collective-permute-start | bytes 884744 | tf_op jit(solution)/shard_map/ppermute | solution.py:21
  114.5 6.5 %copy-start.1 = (bf16[20,3072]{1,0:T(8,128)(2,1)}, bf16[20,3072]{1,0:T(8,128)(2,1)S(1)}, u32[]{:S(2)}) copy-start(bf16[20,3072]{1,0:T(8,128)(2,1)S(1)} %reshape.53.gate) | copy-start | bytes 368644
  114.6 4.9 %collective-permute-start.13 = (bf16[4,2,192,384]{3,2,1,0:T(8,128)(2,1)S(1)}, bf16[4,2,192,384]{3,2,1,0:T(8,128)(2,1)S(1)}, u32[]{:S(2)}, u32[]{:S(2)}) collective-permute-start(bf16[4,2,192,384]{3,2,1,0:T(8,128)(2,1)S(1)} %stack.13), channel_id=1, source_target_pairs={{0,64},{64,0},{1,65},{65,1},{2,66},{66,2},{3,67},{67,3},{4,68},{68... | collective-permute-start | bytes 3538952 | tf_op jit(solution)/shard_map/ppermute | solution.py:16
